TPU v7x, 128 devices: a whole 4x4x4 slice. The times are simulated.
128 devices in a mesh: dp: 16 (over y, z), tensor: 8 (over x, core).
Axes of the slice: x: 4, y: 4, z: 4, core: 2. Of those that a mesh axis runs over, the one named last changes fastest.
Arguments:
- hidden_in: bfloat16 [9216, 8192], P(('dp', 'tensor')), may hold values from -600 to 600
- norm_gain: float32 [8192], replicated, may hold values from 0.1 to 1.9
- query_weight: bfloat16 [8192, 4096], P('dp', 'tensor'), may hold values from -0.0625 to 0.0625
- keyval_weight: bfloat16 [8192, 2, 1024], P('dp', None, 'tensor'), may hold values from -0.0625 to 0.0625
- query_bias: float32 [4096], P('tensor'), may hold values from -40 to 40
- keyval_bias: float32 [2, 1024], P(None, 'tensor'), may hold values from -40 to 40
- out_weight: bfloat16 [4096, 8192], P('tensor', 'dp'), may hold values from -0.09375 to 0.09375
- bundle_row_lengths: int32 [16], replicated, may hold values from 1 to 72, as said below
- move_plan: int32 [16], replicated, may hold values from 0 to 15, each once
- first_len: int32 [16, 16], replicated, may hold values from 1 to 72, as said below
Outputs:
- attended: bfloat16 [9216, 8192], P(('dp', 'tensor'))
Inputs may be any that keep to these rules, and one draw needn't show every extreme that they name: `bundle_row_lengths`: the lengths sum to 576; exactly one of them is 72. `move_plan`: each value appears once. first_len[h, b] is at least 1 and at most bundle_row_lengths[b].
All inputs are finite; a program needn't handle non-finite values.
Results may differ from a plain program's by a relative error of at most 0.024.
Values may be sent and summed in bfloat16 or wider, within the bound.
No kernel may reach another device: no remote copies, remote signals or barrier semaphores. Data moves between devices by JAX's collectives and lax.ppermute only.
A program may use at most 128 MiB of HBM per device.

v0:
```python
import functools

import jax
import jax.numpy as jnp
from jax import lax
from jax.experimental import pallas as pl
from jax.experimental.pallas import tpu as pltpu
from jax.sharding import Mesh, PartitionSpec as P

HD = 128
THETA = 1000000.0
EPS = 1e-06
BF = jnp.bfloat16
F32 = jnp.float32
DP = ("y", "z")


def ring(n, step):
    return [(i, (i + step) % n) for i in range(n)]


def hop(v, axis, step):
    with jax.named_scope(f"{axis}{step % lax.axis_size(axis)}"):
        return lax.ppermute(v, axis, ring(lax.axis_size(axis), step))


def swap(v):
    with jax.named_scope("core"):
        return lax.ppermute(v, "c", [(0, 1), (1, 0)])


def after(*values):
    return lax.optimization_barrier(values)


def dot(a, b):
    return jnp.dot(a, b, preferred_element_type=F32)


def attend_kernel(here, heads, core_ref, sum_ref, m_ref, p_ref, bias_ref, cos_ref, sin_ref, back_ref,
                  place_ref, send_ref, out_ref, proj, keys, vals, context):
    rows = sum_ref.shape[0]
    q_cols = heads * HD
    proj[...] = sum_ref[...] + m_ref[...].astype(F32) + p_ref[...].astype(F32) + bias_ref[...]

    def turned(u, at):
        swapped = jnp.concatenate([u[:, HD // 2 :], u[:, : HD // 2]], axis=1)
        return u * cos_ref[at, :] + swapped * sin_ref[at, :]

    every = pl.ds(0, rows)
    keys[...] = turned(proj[:, q_cols : q_cols + HD], every).astype(BF).astype(F32)
    vals[...] = proj[:, q_cols + HD :].astype(BF).astype(F32)
    core = core_ref[0]
    chips = rows // (2 * here)
    lane = lax.broadcasted_iota(jnp.int32, (here, 2 * here), 1)
    own = here + lax.broadcasted_iota(jnp.int32, (here, 2 * here), 0)
    for k in range(2):
        c = core if k == 0 else 1 - core
        for s in range(chips):
            at = pl.ds((k * chips + s) * here, here)
            before = pl.ds(pl.multiple_of(((1 - k) * chips + lax.rem(s + 1 - c, chips)) * here, 8), here)
            ks = jnp.concatenate([keys[before, :], keys[at, :]], axis=0).astype(BF)
            vs = jnp.concatenate([vals[before, :], vals[at, :]], axis=0).astype(BF)
            q = jnp.concatenate(
                [turned(proj[at, h * HD : (h + 1) * HD], at) for h in range(heads)], axis=0
            ).astype(BF)
            scores = lax.dot_general(q, ks, (((1,), (1,)), ((), ())), preferred_element_type=F32)
            allowed = (lane <= own) & (lane >= own - back_ref[at, :])
            allowed = jnp.concatenate([allowed.astype(jnp.int32)] * heads, axis=0) > 0
            scores = jnp.where(allowed, scores * HD ** (-0.5), -jnp.inf)
            e = jnp.exp(scores - jnp.max(scores, axis=1, keepdims=True))
            probs = (e / jnp.sum(e, axis=1, keepdims=True)).astype(BF)
            ctx = jnp.dot(probs, vs, preferred_element_type=F32)
            for h in range(heads):
                context[at, h * HD : (h + 1) * HD] = ctx[h * here : (h + 1) * here]
    ctx = context[...].astype(BF)
    step = out_ref.shape[0] // 4
    for i in range(4):
        at = pl.ds(i * step, step)
        pick = jnp.where(send_ref[at, :] == place_ref[...], 1.0, 0.0).astype(BF)
        out_ref[at, :] = jnp.dot(pick, ctx, preferred_element_type=F32).astype(BF)


def attend(here, heads, slots, core, total, part_m, part_p, bias, cosines, sines, back, places, send_rows):
    rows, cols = total.shape
    vmem = pl.BlockSpec(memory_space=pltpu.VMEM)
    return pl.pallas_call(
        functools.partial(attend_kernel, here, heads),
        out_shape=jax.ShapeDtypeStruct((slots, heads * HD), BF),
        in_specs=[pl.BlockSpec(memory_space=pltpu.SMEM)] + [vmem] * 9,
        out_specs=vmem,
        scratch_shapes=[
            pltpu.VMEM((rows, cols), F32),
            pltpu.VMEM((rows, HD), F32),
            pltpu.VMEM((rows, HD), F32),
            pltpu.VMEM((rows, heads * HD), F32),
        ],
        compiler_params=pltpu.CompilerParams(vmem_limit_bytes=40 * 1024 * 1024),
        cost_estimate=pl.CostEstimate(flops=1 << 30, bytes_accessed=8 << 20, transcendentals=1 << 20),
    )(core, total, part_m, part_p, bias, cosines, sines, back, places, send_rows)


def multiply_kernel(sizes, w_ref, *refs):
    at = 0
    outs = refs[sum(sizes) :]
    for count, out_ref in zip(sizes, outs):
        total, depth = 0.0, 0
        for ref in refs[at : at + count]:
            total += jnp.dot(
                ref[...], w_ref[depth : depth + ref.shape[1]], preferred_element_type=F32
            )
            depth += ref.shape[1]
        out_ref[...] = total
        at += count


def multiply(products, w):
    flat = [t for pieces in products for t in pieces]
    vmem = pl.BlockSpec(memory_space=pltpu.VMEM)
    return pl.pallas_call(
        functools.partial(multiply_kernel, [len(pieces) for pieces in products]),
        out_shape=[jax.ShapeDtypeStruct((p[0].shape[0], w.shape[1]), F32) for p in products],
        in_specs=[vmem] * (1 + len(flat)),
        out_specs=[vmem] * len(products),
        compiler_params=pltpu.CompilerParams(vmem_limit_bytes=32 * 1024 * 1024),
        cost_estimate=pl.CostEstimate(flops=1 << 20, bytes_accessed=1 << 12, transcendentals=0),
    )(w, *flat)


def project_out_kernel(mine_ref, theirs_ref, w_ref, out_ref):
    both = jnp.concatenate([mine_ref[...], theirs_ref[...]], axis=1)
    w = jnp.concatenate([w_ref[i] for i in range(w_ref.shape[0])], axis=1)
    out_ref[...] = jnp.dot(both, w, preferred_element_type=F32).astype(BF)


def project_out(first, count, mine, theirs, w):
    rows, depth = mine.shape
    _, deep, width = w.shape
    group = 2
    whole = pl.BlockSpec((rows, depth), lambda d: (0, 0))
    return pl.pallas_call(
        project_out_kernel,
        out_shape=jax.ShapeDtypeStruct((rows, count * width), BF),
        grid=(count // group,),
        in_specs=[whole, whole, pl.BlockSpec((group, deep, width), lambda d: (first // group + d, 0, 0))],
        out_specs=pl.BlockSpec((rows, group * width), lambda d: (0, d)),
        compiler_params=pltpu.CompilerParams(vmem_limit_bytes=48 * 1024 * 1024),
        cost_estimate=pl.CostEstimate(
            flops=2 * rows * deep * width * count, bytes_accessed=8 << 20, transcendentals=0
        ),
    )(mine, theirs, w)


def interleave_kernel(side, width, at_ref, *refs):
    *parts, out_ref = refs
    core, y = at_ref[0], at_ref[1]
    blocks = parts[0].shape[1] // width
    for j in range(len(parts) // 2):
        for i in range(blocks):
            z, back = divmod(j * blocks + i, side)
            at = lax.rem(y + side - back, side) * side + z
            for part, c in ((parts[2 * j], core), (parts[2 * j + 1], 1 - core)):
                to = pl.multiple_of((at * 2 + c) * width, width)
                out_ref[:, pl.ds(to, width)] = part[:, i * width : (i + 1) * width]


def interleave(side, width, at, parts):
    rows, cols = parts[0].shape
    vmem = pl.BlockSpec(memory_space=pltpu.VMEM)
    return pl.pallas_call(
        functools.partial(interleave_kernel, side, width),
        out_shape=jax.ShapeDtypeStruct((rows, cols * len(parts)), BF),
        in_specs=[pl.BlockSpec(memory_space=pltpu.SMEM)] + [vmem] * len(parts),
        out_specs=vmem,
    )(at, *parts)


def shards(
    hidden_in,
    norm_gain,
    query_weight,
    keyval_weight,
    query_bias,
    keyval_bias,
    out_weight,
    lengths,
    move_plan,
    first_len,
):
    packs = lax.axis_size(DP)
    pack = lax.axis_index(DP)
    x = lax.axis_index("x")
    y = lax.axis_index("y")
    core = lax.axis_index("c")
    nx = lax.axis_size("x")
    ny = lax.axis_size("y")
    z = lax.axis_index("z")
    nz = lax.axis_size("z")
    here = hidden_in.shape[0]
    width = hidden_in.shape[1]
    rows = here * nx * 2
    q_cols = query_weight.shape[1]

    r = jnp.arange(here, dtype=jnp.int32)
    places = jnp.concatenate(
        [
            here * (2 * ((x - s) % nx) + (core if k == 0 else 1 - core)) + r
            for k in range(2)
            for s in range(4)
        ]
    )
    places_out = jnp.concatenate(
        [here * (2 * ((x - s) % nx) + k) + r for s in range(4) for k in range(2)]
    )

    ids = jnp.arange(lengths.shape[0], dtype=jnp.int32)
    offsets = jnp.cumsum(lengths) - lengths
    bundle = jnp.sum((places[:, None] >= offsets[None, :]).astype(jnp.int32), axis=1) - 1
    selector = (bundle[:, None] == ids[None, :]).astype(jnp.int32)
    starts = jnp.sum(selector * offsets[None, :], axis=1)
    first_here = jnp.sum(first_len * (jnp.arange(packs)[:, None] == pack).astype(jnp.int32), axis=0)
    splits = jnp.sum(selector * first_here[None, :], axis=1)
    back = places - starts
    back = back - jnp.where(back >= splits, splits, 0)
    indices = jnp.arange(HD // 2, dtype=F32)
    angles = back.astype(F32)[:, None] * (THETA ** (-2.0 * indices / HD))[None, :]
    cosines, sines = jnp.cos(angles), jnp.sin(angles)
    cosines = jnp.concatenate([cosines, cosines], axis=1)
    sines = jnp.concatenate([-sines, sines], axis=1)

    combined = jnp.concatenate([query_weight, keyval_weight.reshape(keyval_weight.shape[0], -1)], axis=1)
    w_in = lax.all_gather(combined, "z", axis=0, tiled=True)
    block = width // ny
    half = block // 2

    values = hidden_in.astype(F32)
    scale = lax.rsqrt(jnp.mean(values * values, axis=1, keepdims=True) + EPS)
    own = (values * scale * norm_gain).astype(BF)

    def features(step):
        return lax.dynamic_slice_in_dim(own, (y + step) % ny * block, block, axis=1)

    pack_0 = features(0)
    with jax.named_scope("exchange"):
        rest = jnp.concatenate(
            [hop(features(2), "y", 2), hop(features(1), "y", 1), hop(features(-1), "y", -1)], axis=0
        )

    cols = out_weight.shape[1] // 2
    w_low, w_high = out_weight[:, :cols], out_weight[:, cols:]
    mine = jnp.where(core == 0, w_low, w_high)
    other = swap(jnp.where(core == 0, w_high, w_low))
    with jax.named_scope("own"):
        left_0, right_0 = hop(pack_0, "x", 1), hop(pack_0, "x", -1)
        low_0, high_0 = hop(left_0[:, :half], "x", 1), hop(right_0[:, half:], "x", -1)
    rest, left_0, right_0, low_0, high_0, cosines, sines = after(
        rest, left_0, right_0, low_0, high_0, cosines, sines
    )

    rest_other = swap(rest)
    w_both, rest_other = after(jnp.concatenate([mine, other], axis=0), rest_other)
    with jax.named_scope("w_out"):
        w_near = jnp.stack([w_both, hop(w_both, "y", 1), hop(w_both, "y", 2), hop(w_both, "y", 3)])

    with jax.named_scope("rest"):
        left, right = hop(rest, "x", 1), hop(rest, "x", -1)
        low, high = hop(left[:, :half], "x", 1), hop(right[:, half:], "x", -1)
    w_near, left, right = after(w_near, left, right)
    w_out = lax.all_gather(w_near, "z", axis=0, tiled=True)

    with jax.named_scope("rest"):
        near = [rest, left, right]
        near_sums = [multiply([[t] for t in side], w_in) for side in (near, [rest_other, swap(left), swap(right)])]
        (low, high), near_sums, mine = after(
            (low, high), near_sums, (pack_0, left_0, low_0, high_0, right_0)
        )
        far_sums = [multiply([side], w_in) for side in ([low, high], [swap(low), swap(high)])]
    with jax.named_scope("own"):
        mine = jnp.concatenate(
            [mine[0], mine[1], jnp.concatenate(mine[2:4], axis=1), mine[4]], axis=0
        )
        sum_0 = jnp.concatenate([dot(mine, w_in), dot(swap(mine), w_in)], axis=0)

    def whole(i):
        at = slice(i * here, (i + 1) * here)
        return jnp.concatenate(
            [t[at] for n, f in zip(near_sums, far_sums) for t in (n[0], n[1], f[0], n[2])], axis=0
        )

    sum_2, sum_m, sum_p = whole(0), whole(1), whole(2)

    mid = sum_0.shape[1] // 2
    two = sum_2.astype(BF)
    a = hop(two[:, :mid], "y", 1)
    b = hop(two[:, mid:], "y", -1)
    up = jnp.concatenate(
        [(sum_p[:, :mid] + a.astype(F32)).astype(BF), sum_p[:, mid:].astype(BF)], axis=1
    )
    down = jnp.concatenate(
        [sum_m[:, :mid].astype(BF), (sum_m[:, mid:] + b.astype(F32)).astype(BF)], axis=1
    )
    from_m = hop(up, "y", 1)
    from_p = hop(down, "y", -1)

    capacity = 2 * rows // packs
    lanes = jnp.arange(capacity, dtype=jnp.int32)
    slots = jnp.arange(packs, dtype=jnp.int32)
    outgoing = (move_plan[None, :] == ((slots - pack) % packs)[:, None]).astype(jnp.int32)
    send_start = jnp.sum(outgoing * offsets[None, :], axis=1)
    send_length = jnp.sum(outgoing * lengths[None, :], axis=1)
    live = lanes[None, :] < send_length[:, None]
    send_rows = jnp.where(live, send_start[:, None] + lanes[None, :], -1).reshape(-1)
    bias = jnp.concatenate([query_bias, keyval_bias.reshape(-1)])[None, :]
    sent = attend(
        here,
        q_cols // HD,
        packs * capacity,
        core.reshape(1),
        sum_0,
        from_m,
        from_p,
        bias,
        cosines,
        sines,
        back[:, None],
        places[None, :],
        send_rows[:, None],
    ).reshape(packs, capacity, q_cols)
    got = lax.all_to_all(sent, DP, split_axis=0, concat_axis=0, tiled=True)
    sources = (pack - move_plan) % packs
    bundle_out = jnp.sum((places_out[:, None] >= offsets[None, :]).astype(jnp.int32), axis=1) - 1
    selector = (bundle_out[:, None] == ids[None, :]).astype(jnp.int32)
    source = jnp.sum(selector * sources[None, :], axis=1)
    slot = source * capacity + places_out - jnp.sum(selector * offsets[None, :], axis=1)
    place = (slot[:, None] == jnp.arange(packs * capacity, dtype=jnp.int32)[None, :]).astype(BF)
    moved = dot(place, got.reshape(packs * capacity, q_cols)).astype(BF)
    theirs = swap(moved)

    parts = []
    pair = 2 * here
    chunks = 2
    count = packs // chunks
    for j in range(chunks):
        partial = project_out(j * count, count, moved, theirs, w_out)
        part = [partial[s * pair : (s + 1) * pair] for s in range(4)]
        mid = part[0].shape[1] // 2
        a = hop(part[2][:, :mid], "x", 1)
        b = hop(part[2][:, mid:], "x", -1)
        up = jnp.concatenate(
            [(part[3][:, :mid].astype(F32) + a.astype(F32)).astype(BF), part[3][:, mid:]], axis=1
        )
        down = jnp.concatenate(
            [part[1][:, :mid], (part[1][:, mid:].astype(F32) + b.astype(F32)).astype(BF)], axis=1
        )
        u, v = hop(up, "x", 1), hop(down, "x", -1)
        total = (part[0].astype(F32) + u.astype(F32) + v.astype(F32)).astype(BF)
        parts.append(jnp.where(core == 0, total[:here], total[here:]))
        parts.append(swap(jnp.where(core == 0, total[here:], total[:here])))
    return interleave(ny, cols, jnp.stack([core, y]), parts)


def solution(mesh):
    packs, tensor = mesh.devices.shape
    side = int(round(packs**0.5))
    fine = Mesh(mesh.devices.reshape(side, packs // side, tensor // 2, 2), ("y", "z", "x", "c"))
    every = ("y", "z", "x", "c")
    heads = ("x", "c")
    in_specs = (
        P(every, None),
        P(),
        P(DP, heads),
        P(DP, None, heads),
        P(heads),
        P(None, heads),
        P(heads, DP),
        P(),
        P(),
        P(),
    )
    return jax.shard_map(
        shards, mesh=fine, in_specs=in_specs, out_specs=P(every, None), check_vma=False
    )
```

profile of v0, /device:TPU:1, one launch (start us, length us, event | category | flops | bytes accessed | tf_op | source)
XLA Modules:
  0.0 224.3 jit_solution(15329561774145970155)
XLA Ops:
  10.4 2.1 collective-permute-start.3
  13.8 3.0 %collective-permute-start = (bf16[72,2048]{1,0:T(8,128)(2,1)}, bf16[72,2048]{1,0:T(8,128)(2,1)S(1)}, u32[]{:S(2)}, u32[]{:S(2)}) collective-permute-start(bf16[72,2048]{1,0:T(8,128)(2,1)} %get-tuple-element.89), channel_id=1, source_target_pairs={{0,64},{32,96},{64,0},{96,32},{1,65},{33,97},{65,1},{97,33},{2,66}... | collective-permute-start | bytes 884744 | tf_op jit(solution)/shard_map/exchange/y2/ppermute | solution.py:24
  17.3 2.3 %collective-permute-start.2 = (bf16[72,2048]{1,0:T(8,128)(2,1)S(1)}, bf16[72,2048]{1,0:T(8,128)(2,1)S(1)}, u32[]{:S(2)}, u32[]{:S(2)}) collective-permute-start(bf16[72,2048]{1,0:T(8,128)(2,1)S(1)} %get-tuple-element.87), channel_id=1, source_target_pairs={{0,96},{32,0},{64,32},{96,64},{1,97},{33,1},{65,33},{97,65},{2,98}... | collective-permute-start | bytes 884744 | tf_op jit(solution)/shard_map/exchange/y3/ppermute | solution.py:24
  25.1 2.7 %collective-permute-start.6 = (bf16[72,1024]{1,0:T(8,128)(2,1)S(1)}, bf16[72,1024]{1,0:T(8,128)(2,1)S(1)}, u32[]{:S(2)}, u32[]{:S(2)}) collective-permute-start(bf16[72,1024]{1,0:T(8,128)(2,1)S(1)} %slice.249), channel_id=1, source_target_pairs={{0,6},{2,0},{4,2},{6,4},{1,7},{3,1},{5,3},{7,5},{8,14},{10,8},{12,... | collective-permute-start | bytes 442376 | tf_op jit(solution)/shard_map/own/x3/ppermute | solution.py:24
  27.8 3.0 %collective-permute-done.1 = bf16[72,2048]{1,0:T(8,128)(2,1)S(1)} collective-permute-done((bf16[72,2048]{1,0:T(8,128)(2,1)}, bf16[72,2048]{1,0:T(8,128)(2,1)S(1)}, u32[]{:S(2)}, u32[]{:S(2)}) %collective-permute-start.1) | collective-permute-done | bytes 294944 | tf_op jit(solution)/shard_map/exchange/y1/ppermute | solution.py:24
  32.3 2.5 %collective-permute-start.12 = (bf16[216,2048]{1,0:T(8,128)(2,1)S(1)}, bf16[216,2048]{1,0:T(8,128)(2,1)}, u32[]{:S(2)}, u32[]{:S(2)}) collective-permute-start(bf16[216,2048]{1,0:T(8,128)(2,1)S(1)} %pad_maximum_fusion.3.refs_0_), channel_id=1, source_target_pairs={{0,1},{1,0},{2,3},{3,2},{4,5},{5,4},{6,7},{7,6},{8,9},{9,8},{10,11... | collective-permute-start | bytes 2654216 | tf_op jit(solution)/shard_map/core/ppermute | solution.py:29
  35.0 2.7 %collective-permute-start.9 = (bf16[216,2048]{1,0:T(8,128)(2,1)S(1)}, bf16[216,2048]{1,0:T(8,128)(2,1)S(1)}, u32[]{:S(2)}, u32[]{:S(2)}) collective-permute-start(bf16[216,2048]{1,0:T(8,128)(2,1)S(1)} %pad_maximum_fusion.3.refs_0_), channel_id=1, source_target_pairs={{0,6},{2,0},{4,2},{6,4},{1,7},{3,1},{5,3},{7,5},{8,14},{10,8},{12,... | collective-permute-start | bytes 2654216 | tf_op jit(solution)/shard_map/rest/x3/ppermute | solution.py:24
  40.5 11.8 %collective-permute-done.13 = bf16[1024,256]{1,0:T(8,128)(2,1)S(1)} collective-permute-done((bf16[1024,256]{1,0:T(8,128)(2,1)S(1)}, bf16[1024,256]{1,0:T(8,128)(2,1)S(1)}, u32[]{:S(2)}, u32[]{:S(2)}) %collective-permute-start.13) | collective-permute-done | bytes 524320 | tf_op jit(solution)/shard_map/w_out/y1/ppermute | solution.py:24
  52.3 9.7 %collective-permute-done.14 = bf16[1024,256]{1,0:T(8,128)(2,1)S(1)} collective-permute-done((bf16[1024,256]{1,0:T(8,128)(2,1)S(1)}, bf16[1024,256]{1,0:T(8,128)(2,1)S(1)}, u32[]{:S(2)}, u32[]{:S(2)}) %collective-permute-start.14) | collective-permute-done | bytes 524320 | tf_op jit(solution)/shard_map/w_out/y2/ppermute | solution.py:24
  64.8 2.2 collective-permute-start.16
  76.1 2.3 %copy-done = bf16[2048,768]{1,0:T(8,128)(2,1)S(1)} copy-done((bf16[2048,768]{1,0:T(8,128)(2,1)S(1)}, bf16[2048,768]{1,0:T(8,128)(2,1)}, u32[]{:S(2)}) %copy-start) | copy-done | bytes 3145752
  78.4 2.3 %rest.4 = (f32[216,768]{1,0:T(8,128)S(1)}, f32[216,768]{1,0:T(8,128)S(1)}, f32[216,768]{1,0:T(8,128)S(1)}) custom-call(bf16[2048,768]{1,0:T(8,128)(2,1)S(1)} %copy-done, bf16[216,2048]{1,0:T(8,128)(2,1)S(1)} %pad_maximum_fusion.3.refs_0_, bf16[216,2048]{1,0:T(8,128)(2,1)S(1)} %collective-permute-done.7.refs_1_, ...), custom_call_target="tpu_custom_call" | custom-call | flops 1048576 | bytes 4096 | tf_op jit(solution)/shard_map/rest/pallas_call | solution.py:120
  80.7 4.3 %rest.5 = (f32[216,768]{1,0:T(8,128)S(1)}, f32[216,768]{1,0:T(8,128)S(1)}, f32[216,768]{1,0:T(8,128)S(1)}) custom-call(bf16[2048,768]{1,0:T(8,128)(2,1)S(1)} %copy-done, bf16[216,2048]{1,0:T(8,128)(2,1)} %collective-permute-done.12.refs_0_, bf16[216,2048]{1,0:T(8,128)(2,1)} %collective-permute-done.16.refs_1_, bf16[216,2048]{1,0:T(8,128)(2,1)} %collective-permute-done.17.refs_2_), custom_call_target="tpu_custom_call" | custom-call | flops 1048576 | bytes 4096 | tf_op jit(solution)/shard_map/rest/pallas_call | solution.py:120
  90.1 2.1 collective-permute-start.23
  92.4 9.6 %collective-permute-done.23 = bf16[576,384]{1,0:T(8,128)(2,1)S(1)} collective-permute-done((bf16[576,384]{1,0:T(8,128)(2,1)S(1)}, bf16[576,384]{1,0:T(8,128)(2,1)S(1)}, u32[]{:S(2)}, u32[]{:S(2)}) %collective-permute-start.23) | collective-permute-done | bytes 442400 | tf_op jit(solution)/shard_map/y3/ppermute | solution.py:24
  102.1 3.3 %collective-permute-start.24 = (bf16[576,768]{1,0:T(8,128)(2,1)S(1)}, bf16[576,768]{1,0:T(8,128)(2,1)S(1)}, u32[]{:S(2)}, u32[]{:S(2)}) collective-permute-start(bf16[576,768]{1,0:T(8,128)(2,1)S(1)} %pad_maximum_fusion.5), channel_id=1, source_target_pairs={{0,96},{32,0},{64,32},{96,64},{1,97},{33,1},{65,33},{97,65},{2,98}... | collective-permute-start | bytes 2654216 | tf_op jit(solution)/shard_map/y3/ppermute | solution.py:24
  108.3 15.4 %collective-permute-done.24.p_ref = bf16[576,768]{1,0:T(8,128)(2,1)S(1)} collective-permute-done((bf16[576,768]{1,0:T(8,128)(2,1)S(1)}, bf16[576,768]{1,0:T(8,128)(2,1)S(1)}, u32[]{:S(2)}, u32[]{:S(2)}) %collective-permute-start.24) | collective-permute-done | bytes 884768 | tf_op jit(solution)/shard_map/y3/ppermute | solution.py:24
  123.7 3.7 %collective-permute-done.22.m_ref = bf16[576,768]{1,0:T(8,128)(2,1)S(1)} collective-permute-done((bf16[576,768]{1,0:T(8,128)(2,1)S(1)}, bf16[576,768]{1,0:T(8,128)(2,1)S(1)}, u32[]{:S(2)}, u32[]{:S(2)}) %collective-permute-start.22) | collective-permute-done | bytes 884768 | tf_op jit(solution)/shard_map/y1/ppermute | solution.py:24
  127.4 7.4 %shard_map.100 = bf16[1152,512]{1,0:T(8,128)(2,1)} custom-call(s32[1]{0:T(128)} %bitcast.core_ref, f32[576,768]{1,0:T(8,128)S(1)} %pad_maximum_fusion.1.sum_ref, bf16[576,768]{1,0:T(8,128)(2,1)S(1)} %collective-permute-done.22.m_ref, bf16[576,768]{1,0:T(8,128)(2,1)S(1)} %collective-permute-done.24.p_ref, f32[1,768]{1,0:T(1,128)S(1)} %broadcast_in_dim.14.bias_ref, ...), custom_call_target="tpu_custom_call" | custom-call | flops 1073741824 | bytes 8388608 | tf_op jit(solution)/shard_map/pallas_call | solution.py:87
  134.8 5.4 %all-to-all-start = ((bf16[16,72,512]{2,1,0:T(8,128)(2,1)}), bf16[16,72,512]{2,1,0:T(8,128)(2,1)S(1)}, u32[]{:S(2)}, u32[]{:S(2)}) async-start(bf16[16,72,512]{2,1,0:T(8,128)(2,1)} %bitcast.16), calls=%async_computation | async-start | bytes 2359296 | tf_op jit(solution)/shard_map/all_to_all | solution.py:329
  140.2 16.2 %all-to-all-done = bf16[16,72,512]{2,1,0:T(8,128)(2,1)S(1)} async-done(((bf16[16,72,512]{2,1,0:T(8,128)(2,1)}), bf16[16,72,512]{2,1,0:T(8,128)(2,1)S(1)}, u32[]{:S(2)}, u32[]{:S(2)}) %all-to-all-start) | async-done | bytes 1179680 | tf_op jit(solution)/shard_map/all_to_all | solution.py:329
  157.4 4.0 %collective-permute-start.25 = (bf16[576,512]{1,0:T(8,128)(2,1)S(1)}, bf16[576,512]{1,0:T(8,128)(2,1)S(1)}, u32[]{:S(2)}, u32[]{:S(2)}) collective-permute-start(bf16[576,512]{1,0:T(8,128)(2,1)S(1)} %fusion.5.mine_ref), channel_id=1, source_target_pairs={{0,1},{1,0},{2,3},{3,2},{4,5},{5,4},{6,7},{7,6},{8,9},{9,8},{10,11... | collective-permute-start | bytes 1769480 | tf_op jit(solution)/shard_map/core/ppermute | solution.py:29
  163.0 5.0 %shard_map.102 = bf16[576,2048]{1,0:T(8,128)(2,1)S(1)} custom-call(bf16[576,512]{1,0:T(8,128)(2,1)S(1)} %fusion.5.mine_ref, bf16[576,512]{1,0:T(8,128)(2,1)S(1)} %collective-permute-done.25.theirs_ref, bf16[16,1024,256]{2,1,0:T(8,128)(2,1)} %all-gather.5.cloned.1.call-done.w_ref), custom_call_target="tpu_custom_call" | custom-call | flops 2415919104 | bytes 8388608 | tf_op jit(solution)/shard_map/pallas_call | solution.py:141
  171.1 5.0 %shard_map.101 = bf16[576,2048]{1,0:T(8,128)(2,1)S(1)} custom-call(bf16[576,512]{1,0:T(8,128)(2,1)S(1)} %fusion.5.mine_ref, bf16[576,512]{1,0:T(8,128)(2,1)S(1)} %collective-permute-done.25.theirs_ref, bf16[16,1024,256]{2,1,0:T(8,128)(2,1)} %all-gather.5.cloned.1.call-done.w_ref), custom_call_target="tpu_custom_call" | custom-call | flops 2415919104 | bytes 8388608 | tf_op jit(solution)/shard_map/pallas_call | solution.py:141
  176.2 2.7 %collective-permute-start.28 = (bf16[144,1024]{1,0:T(8,128)(2,1)S(1)}, bf16[144,1024]{1,0:T(8,128)(2,1)S(1)}, u32[]{:S(2)}, u32[]{:S(2)}) collective-permute-start(bf16[144,1024]{1,0:T(8,128)(2,1)S(1)} %get-tuple-element.83), channel_id=1, source_target_pairs={{0,6},{2,0},{4,2},{6,4},{1,7},{3,1},{5,3},{7,5},{8,14},{10,8},{12,... | collective-permute-start | bytes 884744 | tf_op jit(solution)/shard_map/x3/ppermute | solution.py:24
  179.3 2.7 %collective-permute-start.34 = (bf16[144,2048]{1,0:T(8,128)(2,1)S(1)}, bf16[144,2048]{1,0:T(8,128)(2,1)S(1)}, u32[]{:S(2)}, u32[]{:S(2)}) collective-permute-start(bf16[144,2048]{1,0:T(8,128)(2,1)S(1)} %pad_maximum_fusion.10), channel_id=1, source_target_pairs={{0,6},{2,0},{4,2},{6,4},{1,7},{3,1},{5,3},{7,5},{8,14},{10,8},{12,... | collective-permute-start | bytes 1769480 | tf_op jit(solution)/shard_map/x3/ppermute | solution.py:24
  182.0 2.8 %collective-permute-done.26 = bf16[144,1024]{1,0:T(8,128)(2,1)S(1)} collective-permute-done((bf16[144,1024]{1,0:T(8,128)(2,1)S(1)}, bf16[144,1024]{1,0:T(8,128)(2,1)S(1)}, u32[]{:S(2)}, u32[]{:S(2)}) %collective-permute-start.26) | collective-permute-done | bytes 294944 | tf_op jit(solution)/shard_map/x1/ppermute | solution.py:24
  185.2 2.7 %collective-permute-start.29 = (bf16[144,2048]{1,0:T(8,128)(2,1)S(1)}, bf16[144,2048]{1,0:T(8,128)(2,1)S(1)}, u32[]{:S(2)}, u32[]{:S(2)}) collective-permute-start(bf16[144,2048]{1,0:T(8,128)(2,1)S(1)} %pad_maximum_fusion.8), channel_id=1, source_target_pairs={{0,6},{2,0},{4,2},{6,4},{1,7},{3,1},{5,3},{7,5},{8,14},{10,8},{12,... | collective-permute-start | bytes 1769480 | tf_op jit(solution)/shard_map/x3/ppermute | solution.py:24
  188.0 9.5 %collective-permute-done.32 = bf16[144,2048]{1,0:T(8,128)(2,1)S(1)} collective-permute-done((bf16[144,2048]{1,0:T(8,128)(2,1)S(1)}, bf16[144,2048]{1,0:T(8,128)(2,1)S(1)}, u32[]{:S(2)}, u32[]{:S(2)}) %collective-permute-start.32) | collective-permute-done | bytes 589856 | tf_op jit(solution)/shard_map/x1/ppermute | solution.py:24
  198.5 3.7 %collective-permute-start.35 = (bf16[72,2048]{1,0:T(8,128)(2,1)S(1)}, bf16[72,2048]{1,0:T(8,128)(2,1)S(1)}, u32[]{:S(2)}, u32[]{:S(2)}) collective-permute-start(bf16[72,2048]{1,0:T(8,128)(2,1)S(1)} %get-tuple-element.108), channel_id=1, source_target_pairs={{0,1},{1,0},{2,3},{3,2},{4,5},{5,4},{6,7},{7,6},{8,9},{9,8},{10,11... | collective-permute-start | bytes 884744 | tf_op jit(solution)/shard_map/core/ppermute | solution.py:29
  202.2 7.9 %collective-permute-done.27 = bf16[144,2048]{1,0:T(8,128)(2,1)S(1)} collective-permute-done((bf16[144,2048]{1,0:T(8,128)(2,1)S(1)}, bf16[144,2048]{1,0:T(8,128)(2,1)S(1)}, u32[]{:S(2)}, u32[]{:S(2)}) %collective-permute-start.27) | collective-permute-done | bytes 589856 | tf_op jit(solution)/shard_map/x1/ppermute | solution.py:24
  215.1 2.4 %shard_map.103 = bf16[72,8192]{1,0:T(8,128)(2,1)} custom-call(s32[2]{0:T(128)} %pad_add_fusion.at_ref, bf16[72,2048]{1,0:T(8,128)(2,1)} %get-tuple-element.111.refs_0_, bf16[72,2048]{1,0:T(8,128)(2,1)} %copy-done.13, bf16[72,2048]{1,0:T(8,128)(2,1)} %get-tuple-element.109.refs_2_, bf16[72,2048]{1,0:T(8,128)(2,1)} %copy-done.12), custom_call_target="tpu_custom_call" | custom-call | tf_op jit(solution)/shard_map/pallas_call | solution.py:170
  (214 shorter events, 47.4 us)
Async XLA Ops:
  6.5 69.5 %all-gather.3.cloned.1.call-start = ((), (), s32[]{:S(2)}) async-start(), calls=%async_computation.1 | async-start | bytes 3932160 | tf_op jit(solution)/shard_map/all_gather | solution.py:232
  10.4 14.6 %collective-permute-start.3 = (bf16[72,2048]{1,0:T(8,128)(2,1)S(1)}, bf16[72,2048]{1,0:T(8,128)(2,1)S(1)}, u32[]{:S(2)}, u32[]{:S(2)}) collective-permute-start(bf16[72,2048]{1,0:T(8,128)(2,1)S(1)} %get-tuple-element.51), channel_id=1, source_target_pairs={{0,2},{2,4},{4,6},{6,0},{1,3},{3,5},{5,7},{7,1},{8,10},{10,12},{12... | collective-permute-start | bytes 884744 | tf_op jit(solution)/shard_map/own/x1/ppermute | solution.py:24
  12.5 12.6 %collective-permute-start.4 = (bf16[72,2048]{1,0:T(8,128)(2,1)S(1)}, bf16[72,2048]{1,0:T(8,128)(2,1)S(1)}, u32[]{:S(2)}, u32[]{:S(2)}) collective-permute-start(bf16[72,2048]{1,0:T(8,128)(2,1)S(1)} %get-tuple-element.51), channel_id=1, source_target_pairs={{0,6},{2,0},{4,2},{6,4},{1,7},{3,1},{5,3},{7,5},{8,14},{10,8},{12,... | collective-permute-start | bytes 884744 | tf_op jit(solution)/shard_map/own/x3/ppermute | solution.py:24
  13.8 14.0 %collective-permute-start = (bf16[72,2048]{1,0:T(8,128)(2,1)}, bf16[72,2048]{1,0:T(8,128)(2,1)S(1)}, u32[]{:S(2)}, u32[]{:S(2)}) collective-permute-start(bf16[72,2048]{1,0:T(8,128)(2,1)} %get-tuple-element.89), channel_id=1, source_target_pairs={{0,64},{32,96},{64,0},{96,32},{1,65},{33,97},{65,1},{97,33},{2,66}... | collective-permute-start | bytes 884744 | tf_op jit(solution)/shard_map/exchange/y2/ppermute | solution.py:24
  16.9 14.0 %collective-permute-start.1 = (bf16[72,2048]{1,0:T(8,128)(2,1)}, bf16[72,2048]{1,0:T(8,128)(2,1)S(1)}, u32[]{:S(2)}, u32[]{:S(2)}) collective-permute-start(bf16[72,2048]{1,0:T(8,128)(2,1)} %get-tuple-element.88), channel_id=1, source_target_pairs={{0,32},{32,64},{64,96},{96,0},{1,33},{33,65},{65,97},{97,1},{2,34}... | collective-permute-start | bytes 884744 | tf_op jit(solution)/shard_map/exchange/y1/ppermute | solution.py:24
  17.3 13.6 %collective-permute-start.2 = (bf16[72,2048]{1,0:T(8,128)(2,1)S(1)}, bf16[72,2048]{1,0:T(8,128)(2,1)S(1)}, u32[]{:S(2)}, u32[]{:S(2)}) collective-permute-start(bf16[72,2048]{1,0:T(8,128)(2,1)S(1)} %get-tuple-element.87), channel_id=1, source_target_pairs={{0,96},{32,0},{64,32},{96,64},{1,97},{33,1},{65,33},{97,65},{2,98}... | collective-permute-start | bytes 884744 | tf_op jit(solution)/shard_map/exchange/y3/ppermute | solution.py:24
  20.6 142.5 %all-gather.5.cloned.1.call-start = ((), (), s32[]{:S(2)}) async-start(), calls=%async_computation.2 | async-start | bytes 10485760 | tf_op jit(solution)/shard_map/all_gather | solution.py:269
  25.1 6.5 %collective-permute-start.6 = (bf16[72,1024]{1,0:T(8,128)(2,1)S(1)}, bf16[72,1024]{1,0:T(8,128)(2,1)S(1)}, u32[]{:S(2)}, u32[]{:S(2)}) collective-permute-start(bf16[72,1024]{1,0:T(8,128)(2,1)S(1)} %slice.249), channel_id=1, source_target_pairs={{0,6},{2,0},{4,2},{6,4},{1,7},{3,1},{5,3},{7,5},{8,14},{10,8},{12,... | collective-permute-start | bytes 442376 | tf_op jit(solution)/shard_map/own/x3/ppermute | solution.py:24
  35.0 29.7 %collective-permute-start.7 = (bf16[216,2048]{1,0:T(8,128)(2,1)S(1)}, bf16[216,2048]{1,0:T(8,128)(2,1)S(1)}, u32[]{:S(2)}, u32[]{:S(2)}) collective-permute-start(bf16[216,2048]{1,0:T(8,128)(2,1)S(1)} %pad_maximum_fusion.3.refs_0_), channel_id=1, source_target_pairs={{0,2},{2,4},{4,6},{6,0},{1,3},{3,5},{5,7},{7,1},{8,10},{10,12},{12... | collective-permute-start | bytes 2654216 | tf_op jit(solution)/shard_map/rest/x1/ppermute | solution.py:24
  35.0 29.7 %collective-permute-start.9 = (bf16[216,2048]{1,0:T(8,128)(2,1)S(1)}, bf16[216,2048]{1,0:T(8,128)(2,1)S(1)}, u32[]{:S(2)}, u32[]{:S(2)}) collective-permute-start(bf16[216,2048]{1,0:T(8,128)(2,1)S(1)} %pad_maximum_fusion.3.refs_0_), channel_id=1, source_target_pairs={{0,6},{2,0},{4,2},{6,4},{1,7},{3,1},{5,3},{7,5},{8,14},{10,8},{12,... | collective-permute-start | bytes 2654216 | tf_op jit(solution)/shard_map/rest/x3/ppermute | solution.py:24
  37.8 14.5 %collective-permute-start.13 = (bf16[1024,256]{1,0:T(8,128)(2,1)S(1)}, bf16[1024,256]{1,0:T(8,128)(2,1)S(1)}, u32[]{:S(2)}, u32[]{:S(2)}) collective-permute-start(bf16[1024,256]{1,0:T(8,128)(2,1)S(1)} %pad_maximum_fusion.11), channel_id=1, source_target_pairs={{0,32},{32,64},{64,96},{96,0},{1,33},{33,65},{65,97},{97,1},{2,34}... | collective-permute-start | bytes 1572872 | tf_op jit(solution)/shard_map/w_out/y1/ppermute | solution.py:24
  37.9 24.2 %collective-permute-start.14 = (bf16[1024,256]{1,0:T(8,128)(2,1)S(1)}, bf16[1024,256]{1,0:T(8,128)(2,1)S(1)}, u32[]{:S(2)}, u32[]{:S(2)}) collective-permute-start(bf16[1024,256]{1,0:T(8,128)(2,1)S(1)} %pad_maximum_fusion.11), channel_id=1, source_target_pairs={{0,64},{32,96},{64,0},{96,32},{1,65},{33,97},{65,1},{97,33},{2,66}... | collective-permute-start | bytes 1572872 | tf_op jit(solution)/shard_map/w_out/y2/ppermute | solution.py:24
  39.8 23.3 %collective-permute-start.15 = (bf16[1024,256]{1,0:T(8,128)(2,1)S(1)}, bf16[1024,256]{1,0:T(8,128)(2,1)S(1)}, u32[]{:S(2)}, u32[]{:S(2)}) collective-permute-start(bf16[1024,256]{1,0:T(8,128)(2,1)S(1)} %pad_maximum_fusion.11), channel_id=1, source_target_pairs={{0,96},{32,0},{64,32},{96,64},{1,97},{33,1},{65,33},{97,65},{2,98}... | collective-permute-start | bytes 1572872 | tf_op jit(solution)/shard_map/w_out/y3/ppermute | solution.py:24
  64.8 15.9 %collective-permute-start.16 = (bf16[216,2048]{1,0:T(8,128)(2,1)S(1)}, bf16[216,2048]{1,0:T(8,128)(2,1)}, u32[]{:S(2)}, u32[]{:S(2)}) collective-permute-start(bf16[216,2048]{1,0:T(8,128)(2,1)S(1)} %collective-permute-done.7.refs_1_), channel_id=1, source_target_pairs={{0,1},{1,0},{2,3},{3,2},{4,5},{5,4},{6,7},{7,6},{8,9},{9,8},{10,11... | collective-permute-start | bytes 2654216 | tf_op jit(solution)/shard_map/rest/core/ppermute | solution.py:29
  67.0 13.7 %collective-permute-start.17 = (bf16[216,2048]{1,0:T(8,128)(2,1)S(1)}, bf16[216,2048]{1,0:T(8,128)(2,1)}, u32[]{:S(2)}, u32[]{:S(2)}) collective-permute-start(bf16[216,2048]{1,0:T(8,128)(2,1)S(1)} %collective-permute-done.9.refs_2_), channel_id=1, source_target_pairs={{0,1},{1,0},{2,3},{3,2},{4,5},{5,4},{6,7},{7,6},{8,9},{9,8},{10,11... | collective-permute-start | bytes 2654216 | tf_op jit(solution)/shard_map/rest/core/ppermute | solution.py:29
  68.8 16.3 %collective-permute-start.10 = (bf16[216,1024]{1,0:T(8,128)(2,1)}, bf16[216,1024]{1,0:T(8,128)(2,1)}, u32[]{:S(2)}, u32[]{:S(2)}) collective-permute-start(bf16[216,1024]{1,0:T(8,128)(2,1)} %slice.251), channel_id=1, source_target_pairs={{0,6},{2,0},{4,2},{6,4},{1,7},{3,1},{5,3},{7,5},{8,14},{10,8},{12,... | collective-permute-start | bytes 1327112 | tf_op jit(solution)/shard_map/rest/x3/ppermute | solution.py:24
  71.5 13.6 %collective-permute-start.8 = (bf16[216,1024]{1,0:T(8,128)(2,1)}, bf16[216,1024]{1,0:T(8,128)(2,1)}, u32[]{:S(2)}, u32[]{:S(2)}) collective-permute-start(bf16[216,1024]{1,0:T(8,128)(2,1)} %slice.250), channel_id=1, source_target_pairs={{0,2},{2,4},{4,6},{6,0},{1,3},{3,5},{5,7},{7,1},{8,10},{10,12},{12... | collective-permute-start | bytes 1327112 | tf_op jit(solution)/shard_map/rest/x1/ppermute | solution.py:24
  86.1 21.0 %collective-permute-start.18 = (bf16[288,2048]{1,0:T(8,128)(2,1)S(1)}, bf16[288,2048]{1,0:T(8,128)(2,1)S(1)}, u32[]{:S(2)}, u32[]{:S(2)}) collective-permute-start(bf16[288,2048]{1,0:T(8,128)(2,1)S(1)} %pad_maximum_fusion.2), channel_id=1, source_target_pairs={{0,1},{1,0},{2,3},{3,2},{4,5},{5,4},{6,7},{7,6},{8,9},{9,8},{10,11... | collective-permute-start | bytes 3538952 | tf_op jit(solution)/shard_map/own/core/ppermute | solution.py:29
  90.1 11.9 %collective-permute-start.23 = (bf16[576,384]{1,0:T(8,128)(2,1)S(1)}, bf16[576,384]{1,0:T(8,128)(2,1)S(1)}, u32[]{:S(2)}, u32[]{:S(2)}) collective-permute-start(bf16[576,384]{1,0:T(8,128)(2,1)S(1)} %get-tuple-element.90), channel_id=1, source_target_pairs={{0,96},{32,0},{64,32},{96,64},{1,97},{33,1},{65,33},{97,65},{2,98}... | collective-permute-start | bytes 1327112 | tf_op jit(solution)/shard_map/y3/ppermute | solution.py:24
  92.2 13.3 %collective-permute-start.21 = (bf16[576,384]{1,0:T(8,128)(2,1)S(1)}, bf16[576,384]{1,0:T(8,128)(2,1)S(1)}, u32[]{:S(2)}, u32[]{:S(2)}) collective-permute-start(bf16[576,384]{1,0:T(8,128)(2,1)S(1)} %get-tuple-element.91), channel_id=1, source_target_pairs={{0,32},{32,64},{64,96},{96,0},{1,33},{33,65},{65,97},{97,1},{2,34}... | collective-permute-start | bytes 1327112 | tf_op jit(solution)/shard_map/y1/ppermute | solution.py:24
  102.1 21.6 %collective-permute-start.24 = (bf16[576,768]{1,0:T(8,128)(2,1)S(1)}, bf16[576,768]{1,0:T(8,128)(2,1)S(1)}, u32[]{:S(2)}, u32[]{:S(2)}) collective-permute-start(bf16[576,768]{1,0:T(8,128)(2,1)S(1)} %pad_maximum_fusion.5), channel_id=1, source_target_pairs={{0,96},{32,0},{64,32},{96,64},{1,97},{33,1},{65,33},{97,65},{2,98}... | collective-permute-start | bytes 2654216 | tf_op jit(solution)/shard_map/y3/ppermute | solution.py:24
  105.7 21.7 %collective-permute-start.22 = (bf16[576,768]{1,0:T(8,128)(2,1)S(1)}, bf16[576,768]{1,0:T(8,128)(2,1)S(1)}, u32[]{:S(2)}, u32[]{:S(2)}) collective-permute-start(bf16[576,768]{1,0:T(8,128)(2,1)S(1)} %pad_maximum_fusion.4), channel_id=1, source_target_pairs={{0,32},{32,64},{64,96},{96,0},{1,33},{33,65},{65,97},{97,1},{2,34}... | collective-permute-start | bytes 2654216 | tf_op jit(solution)/shard_map/y1/ppermute | solution.py:24
  134.8 21.6 %all-to-all-start = ((bf16[16,72,512]{2,1,0:T(8,128)(2,1)}), bf16[16,72,512]{2,1,0:T(8,128)(2,1)S(1)}, u32[]{:S(2)}, u32[]{:S(2)}) async-start(bf16[16,72,512]{2,1,0:T(8,128)(2,1)} %bitcast.16), calls=%async_computation | async-start | bytes 2359296 | tf_op jit(solution)/shard_map/all_to_all | solution.py:329
  168.1 10.8 %collective-permute-start.31 = (bf16[144,1024]{1,0:T(8,128)(2,1)S(1)}, bf16[144,1024]{1,0:T(8,128)(2,1)S(1)}, u32[]{:S(2)}, u32[]{:S(2)}) collective-permute-start(bf16[144,1024]{1,0:T(8,128)(2,1)S(1)} %get-tuple-element.76), channel_id=1, source_target_pairs={{0,2},{2,4},{4,6},{6,0},{1,3},{3,5},{5,7},{7,1},{8,10},{10,12},{12... | collective-permute-start | bytes 884744 | tf_op jit(solution)/shard_map/x1/ppermute | solution.py:24
  169.4 9.5 %collective-permute-start.33 = (bf16[144,1024]{1,0:T(8,128)(2,1)S(1)}, bf16[144,1024]{1,0:T(8,128)(2,1)S(1)}, u32[]{:S(2)}, u32[]{:S(2)}) collective-permute-start(bf16[144,1024]{1,0:T(8,128)(2,1)S(1)} %get-tuple-element.77), channel_id=1, source_target_pairs={{0,6},{2,0},{4,2},{6,4},{1,7},{3,1},{5,3},{7,5},{8,14},{10,8},{12,... | collective-permute-start | bytes 884744 | tf_op jit(solution)/shard_map/x3/ppermute | solution.py:24
  176.1 8.7 %collective-permute-start.26 = (bf16[144,1024]{1,0:T(8,128)(2,1)S(1)}, bf16[144,1024]{1,0:T(8,128)(2,1)S(1)}, u32[]{:S(2)}, u32[]{:S(2)}) collective-permute-start(bf16[144,1024]{1,0:T(8,128)(2,1)S(1)} %get-tuple-element.82), channel_id=1, source_target_pairs={{0,2},{2,4},{4,6},{6,0},{1,3},{3,5},{5,7},{7,1},{8,10},{10,12},{12... | collective-permute-start | bytes 884744 | tf_op jit(solution)/shard_map/x1/ppermute | solution.py:24
  176.2 8.6 %collective-permute-start.28 = (bf16[144,1024]{1,0:T(8,128)(2,1)S(1)}, bf16[144,1024]{1,0:T(8,128)(2,1)S(1)}, u32[]{:S(2)}, u32[]{:S(2)}) collective-permute-start(bf16[144,1024]{1,0:T(8,128)(2,1)S(1)} %get-tuple-element.83), channel_id=1, source_target_pairs={{0,6},{2,0},{4,2},{6,4},{1,7},{3,1},{5,3},{7,5},{8,14},{10,8},{12,... | collective-permute-start | bytes 884744 | tf_op jit(solution)/shard_map/x3/ppermute | solution.py:24
  179.2 18.3 %collective-permute-start.32 = (bf16[144,2048]{1,0:T(8,128)(2,1)S(1)}, bf16[144,2048]{1,0:T(8,128)(2,1)S(1)}, u32[]{:S(2)}, u32[]{:S(2)}) collective-permute-start(bf16[144,2048]{1,0:T(8,128)(2,1)S(1)} %pad_maximum_fusion.9), channel_id=1, source_target_pairs={{0,2},{2,4},{4,6},{6,0},{1,3},{3,5},{5,7},{7,1},{8,10},{10,12},{12... | collective-permute-start | bytes 1769480 | tf_op jit(solution)/shard_map/x1/ppermute | solution.py:24
  179.3 18.2 %collective-permute-start.34 = (bf16[144,2048]{1,0:T(8,128)(2,1)S(1)}, bf16[144,2048]{1,0:T(8,128)(2,1)S(1)}, u32[]{:S(2)}, u32[]{:S(2)}) collective-permute-start(bf16[144,2048]{1,0:T(8,128)(2,1)S(1)} %pad_maximum_fusion.10), channel_id=1, source_target_pairs={{0,6},{2,0},{4,2},{6,4},{1,7},{3,1},{5,3},{7,5},{8,14},{10,8},{12,... | collective-permute-start | bytes 1769480 | tf_op jit(solution)/shard_map/x3/ppermute | solution.py:24
  185.1 25.0 %collective-permute-start.27 = (bf16[144,2048]{1,0:T(8,128)(2,1)S(1)}, bf16[144,2048]{1,0:T(8,128)(2,1)S(1)}, u32[]{:S(2)}, u32[]{:S(2)}) collective-permute-start(bf16[144,2048]{1,0:T(8,128)(2,1)S(1)} %pad_maximum_fusion.7), channel_id=1, source_target_pairs={{0,2},{2,4},{4,6},{6,0},{1,3},{3,5},{5,7},{7,1},{8,10},{10,12},{12... | collective-permute-start | bytes 1769480 | tf_op jit(solution)/shard_map/x1/ppermute | solution.py:24
  185.2 24.9 %collective-permute-start.29 = (bf16[144,2048]{1,0:T(8,128)(2,1)S(1)}, bf16[144,2048]{1,0:T(8,128)(2,1)S(1)}, u32[]{:S(2)}, u32[]{:S(2)}) collective-permute-start(bf16[144,2048]{1,0:T(8,128)(2,1)S(1)} %pad_maximum_fusion.8), channel_id=1, source_target_pairs={{0,6},{2,0},{4,2},{6,4},{1,7},{3,1},{5,3},{7,5},{8,14},{10,8},{12,... | collective-permute-start | bytes 1769480 | tf_op jit(solution)/shard_map/x3/ppermute | solution.py:24
  198.5 15.3 %collective-permute-start.35 = (bf16[72,2048]{1,0:T(8,128)(2,1)S(1)}, bf16[72,2048]{1,0:T(8,128)(2,1)S(1)}, u32[]{:S(2)}, u32[]{:S(2)}) collective-permute-start(bf16[72,2048]{1,0:T(8,128)(2,1)S(1)} %get-tuple-element.108), channel_id=1, source_target_pairs={{0,1},{1,0},{2,3},{3,2},{4,5},{5,4},{6,7},{7,6},{8,9},{9,8},{10,11... | collective-permute-start | bytes 884744 | tf_op jit(solution)/shard_map/core/ppermute | solution.py:29
  (38 other events, 241.0 us)
Sparse Core Ops, SparseCore 0:
  20.7 39.7 all-gather.2
  64.9 98.1 all-gather.4
where the time goes:
time: 225 us; the launch traced here: 224 us
  waiting for transfers between devices  93 us (41%)
  starting transfers between devices  57.7 us (26%)
  Pallas kernels  29.3 us (13%)
  other arithmetic  16.7 us (7%)
  between operations  14.5 us (6%)
  local copies, waits for them, and re-layouts  10 us (4%)
  matrix products  3.14 us (1%)
    ppermute x26, waiting for transfers between devices, hop(): return lax.ppermute(v, axis, ring(lax.axis_size(axis), step))  74.5 us
    ppermute x26, starting transfers between devices, hop(): return lax.ppermute(v, axis, ring(lax.axis_size(axis), step))  36.4 us
    all_to_all x1, waiting for transfers between devices, shards(): got = lax.all_to_all(sent, DP, split_axis=0, concat_axis=0, tiled=True)  16.2 us
    ppermute x10, starting transfers between devices, swap(): return lax.ppermute(v, 'c', [(0, 1), (1, 0)])  15.9 us
    pallas_call x2, Pallas kernels, project_out(): pl.pallas_call(project_out_kernel, out_shape=jax.ShapeDtypeStruct((rows,...  9.96 us
    pallas_call x4, Pallas kernels, multiply(): pl.pallas_call(functools.partial(multiply_kernel, [len(pieces) for pieces...  9.52 us
    pallas_call x1, Pallas kernels, attend(): pl.pallas_call(functools.partial(attend_kernel, here, heads), out_shape=j...  7.39 us
    all_to_all x1, starting transfers between devices, shards(): got = lax.all_to_all(sent, DP, split_axis=0, concat_axis=0, tiled=True)  5.37 us
  transfers between devices with their start and end apart: 39, of which 14 were waited for; matrix products, arithmetic and copies ran while one was open for 10% of the time, Pallas kernels for 10%

commit v1 on v0

--- a/solution.py
+++ b/solution.py
@@ -229,6 +229,7 @@
     sines = jnp.concatenate([-sines, sines], axis=1)
 
     combined = jnp.concatenate([query_weight, keyval_weight.reshape(keyval_weight.shape[0], -1)], axis=1)
+    hidden_in, combined = after(hidden_in, combined)
     w_in = lax.all_gather(combined, "z", axis=0, tiled=True)
     block = width // ny
     half = block // 2
@@ -253,12 +254,12 @@
     with jax.named_scope("own"):
         left_0, right_0 = hop(pack_0, "x", 1), hop(pack_0, "x", -1)
         low_0, high_0 = hop(left_0[:, :half], "x", 1), hop(right_0[:, half:], "x", -1)
-    rest, left_0, right_0, low_0, high_0, cosines, sines = after(
-        rest, left_0, right_0, low_0, high_0, cosines, sines
+    w_both = jnp.concatenate([mine, other], axis=0)
+    rest, left_0, right_0, low_0, high_0, cosines, sines, w_both = after(
+        rest, left_0, right_0, low_0, high_0, cosines, sines, w_both
     )
 
     rest_other = swap(rest)
-    w_both, rest_other = after(jnp.concatenate([mine, other], axis=0), rest_other)
     with jax.named_scope("w_out"):
         w_near = jnp.stack([w_both, hop(w_both, "y", 1), hop(w_both, "y", 2), hop(w_both, "y", 3)])
 

time: 225 us -> 225 us (level)
  transfers between devices with their start and end apart: 39 -> 39, of which waited for: 14 -> 16; matrix products, arithmetic and copies ran while one was open for 10% -> 10% of each run, Pallas kernels for 10% -> 10%
where the time goes in v1:
time: 225 us; the launch traced here: 224 us
  waiting for transfers between devices  93.6 us (42%)
  starting transfers between devices  56.8 us (25%)
  Pallas kernels  29.2 us (13%)
  other arithmetic  16.6 us (7%)
  between operations  14.4 us (6%)
  local copies, waits for them, and re-layouts  10.4 us (5%)
  matrix products  3.14 us (1%)
    ppermute x26, waiting for transfers between devices, hop(): return lax.ppermute(v, axis, ring(lax.axis_size(axis), step))  75.1 us
    ppermute x26, starting transfers between devices, hop(): return lax.ppermute(v, axis, ring(lax.axis_size(axis), step))  36.2 us
    all_to_all x1, waiting for transfers between devices, shards(): got = lax.all_to_all(sent, DP, split_axis=0, concat_axis=0, tiled=True)  16.1 us
    ppermute x10, starting transfers between devices, swap(): return lax.ppermute(v, 'c', [(0, 1), (1, 0)])  15.5 us
    pallas_call x2, Pallas kernels, project_out(): pl.pallas_call(project_out_kernel, out_shape=jax.ShapeDtypeStruct((rows,...  9.96 us
    pallas_call x4, Pallas kernels, multiply(): pl.pallas_call(functools.partial(multiply_kernel, [len(pieces) for pieces...  9.51 us
    pallas_call x1, Pallas kernels, attend(): pl.pallas_call(functools.partial(attend_kernel, here, heads), out_shape=j...  7.38 us
    unnamed x77, local copies, waits for them, and re-layouts  5.21 us
  transfers between devices with their start and end apart: 39, of which 16 were waited for; matrix products, arithmetic and copies ran while one was open for 10% of the time, Pallas kernels for 10%

profile of v1, /device:TPU:1, one launch (start us, length us, event | category | flops | bytes accessed | tf_op | source)
XLA Modules:
  0.0 224.2 jit_solution(7206819441153247287)
XLA Ops:
  11.5 2.0 collective-permute-start.3
  14.8 3.1 %collective-permute-start = (bf16[72,2048]{1,0:T(8,128)(2,1)}, bf16[72,2048]{1,0:T(8,128)(2,1)S(1)}, u32[]{:S(2)}, u32[]{:S(2)}) collective-permute-start(bf16[72,2048]{1,0:T(8,128)(2,1)} %get-tuple-element.91), channel_id=1, source_target_pairs={{0,64},{32,96},{64,0},{96,32},{1,65},{33,97},{65,1},{97,33},{2,66}... | collective-permute-start | bytes 884744 | tf_op jit(solution)/shard_map/exchange/y2/ppermute | solution.py:24
  23.5 2.4 %collective-permute-start.2 = (bf16[72,2048]{1,0:T(8,128)(2,1)}, bf16[72,2048]{1,0:T(8,128)(2,1)S(1)}, u32[]{:S(2)}, u32[]{:S(2)}) collective-permute-start(bf16[72,2048]{1,0:T(8,128)(2,1)} %get-tuple-element.89), channel_id=1, source_target_pairs={{0,96},{32,0},{64,32},{96,64},{1,97},{33,1},{65,33},{97,65},{2,98}... | collective-permute-start | bytes 884744 | tf_op jit(solution)/shard_map/exchange/y3/ppermute | solution.py:24
  28.0 2.7 %collective-permute-start.6 = (bf16[72,1024]{1,0:T(8,128)(2,1)S(1)}, bf16[72,1024]{1,0:T(8,128)(2,1)S(1)}, u32[]{:S(2)}, u32[]{:S(2)}) collective-permute-start(bf16[72,1024]{1,0:T(8,128)(2,1)S(1)} %slice.249), channel_id=1, source_target_pairs={{0,6},{2,0},{4,2},{6,4},{1,7},{3,1},{5,3},{7,5},{8,14},{10,8},{12,... | collective-permute-start | bytes 442376 | tf_op jit(solution)/shard_map/own/x3/ppermute | solution.py:24
  36.8 2.5 %collective-permute-start.13 = (bf16[1024,256]{1,0:T(8,128)(2,1)S(1)}, bf16[1024,256]{1,0:T(8,128)(2,1)S(1)}, u32[]{:S(2)}, u32[]{:S(2)}) collective-permute-start(bf16[1024,256]{1,0:T(8,128)(2,1)S(1)} %pad_maximum_fusion.11), channel_id=1, source_target_pairs={{0,64},{32,96},{64,0},{96,32},{1,65},{33,97},{65,1},{97,33},{2,66}... | collective-permute-start | bytes 1572872 | tf_op jit(solution)/shard_map/w_out/y2/ppermute | solution.py:24
  39.5 10.4 %collective-permute-done.12 = bf16[1024,256]{1,0:T(8,128)(2,1)S(1)} collective-permute-done((bf16[1024,256]{1,0:T(8,128)(2,1)S(1)}, bf16[1024,256]{1,0:T(8,128)(2,1)S(1)}, u32[]{:S(2)}, u32[]{:S(2)}) %collective-permute-start.12) | collective-permute-done | bytes 524320 | tf_op jit(solution)/shard_map/w_out/y1/ppermute | solution.py:24
  49.9 11.4 %collective-permute-done.13 = bf16[1024,256]{1,0:T(8,128)(2,1)S(1)} collective-permute-done((bf16[1024,256]{1,0:T(8,128)(2,1)S(1)}, bf16[1024,256]{1,0:T(8,128)(2,1)S(1)}, u32[]{:S(2)}, u32[]{:S(2)}) %collective-permute-start.13) | collective-permute-done | bytes 524320 | tf_op jit(solution)/shard_map/w_out/y2/ppermute | solution.py:24
  63.7 2.3 %collective-permute-start.15 = (bf16[216,2048]{1,0:T(8,128)(2,1)S(1)}, bf16[216,2048]{1,0:T(8,128)(2,1)}, u32[]{:S(2)}, u32[]{:S(2)}) collective-permute-start(bf16[216,2048]{1,0:T(8,128)(2,1)S(1)} %pad_maximum_fusion.3.refs_0_), channel_id=1, source_target_pairs={{0,1},{1,0},{2,3},{3,2},{4,5},{5,4},{6,7},{7,6},{8,9},{9,8},{10,11... | collective-permute-start | bytes 2654216 | tf_op jit(solution)/shard_map/core/ppermute | solution.py:29
  68.2 2.7 %collective-permute-start.11 = (bf16[216,1024]{1,0:T(8,128)(2,1)}, bf16[216,1024]{1,0:T(8,128)(2,1)}, u32[]{:S(2)}, u32[]{:S(2)}) collective-permute-start(bf16[216,1024]{1,0:T(8,128)(2,1)} %slice.251), channel_id=1, source_target_pairs={{0,6},{2,0},{4,2},{6,4},{1,7},{3,1},{5,3},{7,5},{8,14},{10,8},{12,... | collective-permute-start | bytes 1327112 | tf_op jit(solution)/shard_map/rest/x3/ppermute | solution.py:24
  76.2 2.3 %copy-done = bf16[2048,768]{1,0:T(8,128)(2,1)S(1)} copy-done((bf16[2048,768]{1,0:T(8,128)(2,1)S(1)}, bf16[2048,768]{1,0:T(8,128)(2,1)}, u32[]{:S(2)}) %copy-start) | copy-done | bytes 3145752
  78.5 2.3 %rest.4 = (f32[216,768]{1,0:T(8,128)S(1)}, f32[216,768]{1,0:T(8,128)S(1)}, f32[216,768]{1,0:T(8,128)S(1)}) custom-call(bf16[2048,768]{1,0:T(8,128)(2,1)S(1)} %copy-done, bf16[216,2048]{1,0:T(8,128)(2,1)S(1)} %pad_maximum_fusion.3.refs_0_, bf16[216,2048]{1,0:T(8,128)(2,1)S(1)} %collective-permute-done.8.refs_1_, ...), custom_call_target="tpu_custom_call" | custom-call | flops 1048576 | bytes 4096 | tf_op jit(solution)/shard_map/rest/pallas_call | solution.py:120
  80.9 4.3 %rest.5 = (f32[216,768]{1,0:T(8,128)S(1)}, f32[216,768]{1,0:T(8,128)S(1)}, f32[216,768]{1,0:T(8,128)S(1)}) custom-call(bf16[2048,768]{1,0:T(8,128)(2,1)S(1)} %copy-done, bf16[216,2048]{1,0:T(8,128)(2,1)} %collective-permute-done.15.refs_0_, bf16[216,2048]{1,0:T(8,128)(2,1)} %collective-permute-done.16.refs_1_, bf16[216,2048]{1,0:T(8,128)(2,1)} %collective-permute-done.17.refs_2_), custom_call_target="tpu_custom_call" | custom-call | flops 1048576 | bytes 4096 | tf_op jit(solution)/shard_map/rest/pallas_call | solution.py:120
  86.6 2.0 rest.6
  90.0 2.1 collective-permute-start.23
  92.3 9.6 %collective-permute-done.23 = bf16[576,384]{1,0:T(8,128)(2,1)S(1)} collective-permute-done((bf16[576,384]{1,0:T(8,128)(2,1)S(1)}, bf16[576,384]{1,0:T(8,128)(2,1)S(1)}, u32[]{:S(2)}, u32[]{:S(2)}) %collective-permute-start.23) | collective-permute-done | bytes 442400 | tf_op jit(solution)/shard_map/y3/ppermute | solution.py:24
  102.1 3.3 %collective-permute-start.24 = (bf16[576,768]{1,0:T(8,128)(2,1)S(1)}, bf16[576,768]{1,0:T(8,128)(2,1)S(1)}, u32[]{:S(2)}, u32[]{:S(2)}) collective-permute-start(bf16[576,768]{1,0:T(8,128)(2,1)S(1)} %pad_maximum_fusion.5), channel_id=1, source_target_pairs={{0,96},{32,0},{64,32},{96,64},{1,97},{33,1},{65,33},{97,65},{2,98}... | collective-permute-start | bytes 2654216 | tf_op jit(solution)/shard_map/y3/ppermute | solution.py:24
  108.3 15.4 %collective-permute-done.24.p_ref = bf16[576,768]{1,0:T(8,128)(2,1)S(1)} collective-permute-done((bf16[576,768]{1,0:T(8,128)(2,1)S(1)}, bf16[576,768]{1,0:T(8,128)(2,1)S(1)}, u32[]{:S(2)}, u32[]{:S(2)}) %collective-permute-start.24) | collective-permute-done | bytes 884768 | tf_op jit(solution)/shard_map/y3/ppermute | solution.py:24
  123.7 3.7 %collective-permute-done.22.m_ref = bf16[576,768]{1,0:T(8,128)(2,1)S(1)} collective-permute-done((bf16[576,768]{1,0:T(8,128)(2,1)S(1)}, bf16[576,768]{1,0:T(8,128)(2,1)S(1)}, u32[]{:S(2)}, u32[]{:S(2)}) %collective-permute-start.22) | collective-permute-done | bytes 884768 | tf_op jit(solution)/shard_map/y1/ppermute | solution.py:24
  127.4 7.4 %shard_map.100 = bf16[1152,512]{1,0:T(8,128)(2,1)} custom-call(s32[1]{0:T(128)} %bitcast.core_ref, f32[576,768]{1,0:T(8,128)S(1)} %pad_maximum_fusion.1.sum_ref, bf16[576,768]{1,0:T(8,128)(2,1)S(1)} %collective-permute-done.22.m_ref, bf16[576,768]{1,0:T(8,128)(2,1)S(1)} %collective-permute-done.24.p_ref, f32[1,768]{1,0:T(1,128)S(1)} %broadcast_in_dim.14.bias_ref, ...), custom_call_target="tpu_custom_call" | custom-call | flops 1073741824 | bytes 8388608 | tf_op jit(solution)/shard_map/pallas_call | solution.py:87
  134.7 5.1 %all-to-all-start = ((bf16[16,72,512]{2,1,0:T(8,128)(2,1)}), bf16[16,72,512]{2,1,0:T(8,128)(2,1)S(1)}, u32[]{:S(2)}, u32[]{:S(2)}) async-start(bf16[16,72,512]{2,1,0:T(8,128)(2,1)} %bitcast.16), calls=%async_computation | async-start | bytes 2359296 | tf_op jit(solution)/shard_map/all_to_all | solution.py:330
  139.9 16.1 %all-to-all-done = bf16[16,72,512]{2,1,0:T(8,128)(2,1)S(1)} async-done(((bf16[16,72,512]{2,1,0:T(8,128)(2,1)}), bf16[16,72,512]{2,1,0:T(8,128)(2,1)S(1)}, u32[]{:S(2)}, u32[]{:S(2)}) %all-to-all-start) | async-done | bytes 1179680 | tf_op jit(solution)/shard_map/all_to_all | solution.py:330
  157.0 4.1 %collective-permute-start.25 = (bf16[576,512]{1,0:T(8,128)(2,1)S(1)}, bf16[576,512]{1,0:T(8,128)(2,1)S(1)}, u32[]{:S(2)}, u32[]{:S(2)}) collective-permute-start(bf16[576,512]{1,0:T(8,128)(2,1)S(1)} %fusion.5.mine_ref), channel_id=1, source_target_pairs={{0,1},{1,0},{2,3},{3,2},{4,5},{5,4},{6,7},{7,6},{8,9},{9,8},{10,11... | collective-permute-start | bytes 1769480 | tf_op jit(solution)/shard_map/core/ppermute | solution.py:29
  162.8 5.0 %shard_map.102 = bf16[576,2048]{1,0:T(8,128)(2,1)S(1)} custom-call(bf16[576,512]{1,0:T(8,128)(2,1)S(1)} %fusion.5.mine_ref, bf16[576,512]{1,0:T(8,128)(2,1)S(1)} %collective-permute-done.25.theirs_ref, bf16[16,1024,256]{2,1,0:T(8,128)(2,1)} %all-gather.5.cloned.1.call-done.w_ref), custom_call_target="tpu_custom_call" | custom-call | flops 2415919104 | bytes 8388608 | tf_op jit(solution)/shard_map/pallas_call | solution.py:141
  170.9 5.0 %shard_map.101 = bf16[576,2048]{1,0:T(8,128)(2,1)S(1)} custom-call(bf16[576,512]{1,0:T(8,128)(2,1)S(1)} %fusion.5.mine_ref, bf16[576,512]{1,0:T(8,128)(2,1)S(1)} %collective-permute-done.25.theirs_ref, bf16[16,1024,256]{2,1,0:T(8,128)(2,1)} %all-gather.5.cloned.1.call-done.w_ref), custom_call_target="tpu_custom_call" | custom-call | flops 2415919104 | bytes 8388608 | tf_op jit(solution)/shard_map/pallas_call | solution.py:141
  176.1 2.7 %collective-permute-start.28 = (bf16[144,1024]{1,0:T(8,128)(2,1)S(1)}, bf16[144,1024]{1,0:T(8,128)(2,1)S(1)}, u32[]{:S(2)}, u32[]{:S(2)}) collective-permute-start(bf16[144,1024]{1,0:T(8,128)(2,1)S(1)} %get-tuple-element.85), channel_id=1, source_target_pairs={{0,6},{2,0},{4,2},{6,4},{1,7},{3,1},{5,3},{7,5},{8,14},{10,8},{12,... | collective-permute-start | bytes 884744 | tf_op jit(solution)/shard_map/x3/ppermute | solution.py:24
  179.1 2.7 %collective-permute-start.34 = (bf16[144,2048]{1,0:T(8,128)(2,1)S(1)}, bf16[144,2048]{1,0:T(8,128)(2,1)S(1)}, u32[]{:S(2)}, u32[]{:S(2)}) collective-permute-start(bf16[144,2048]{1,0:T(8,128)(2,1)S(1)} %pad_maximum_fusion.10), channel_id=1, source_target_pairs={{0,6},{2,0},{4,2},{6,4},{1,7},{3,1},{5,3},{7,5},{8,14},{10,8},{12,... | collective-permute-start | bytes 1769480 | tf_op jit(solution)/shard_map/x3/ppermute | solution.py:24
  181.9 2.8 %collective-permute-done.26 = bf16[144,1024]{1,0:T(8,128)(2,1)S(1)} collective-permute-done((bf16[144,1024]{1,0:T(8,128)(2,1)S(1)}, bf16[144,1024]{1,0:T(8,128)(2,1)S(1)}, u32[]{:S(2)}, u32[]{:S(2)}) %collective-permute-start.26) | collective-permute-done | bytes 294944 | tf_op jit(solution)/shard_map/x1/ppermute | solution.py:24
  185.1 2.7 %collective-permute-start.29 = (bf16[144,2048]{1,0:T(8,128)(2,1)S(1)}, bf16[144,2048]{1,0:T(8,128)(2,1)S(1)}, u32[]{:S(2)}, u32[]{:S(2)}) collective-permute-start(bf16[144,2048]{1,0:T(8,128)(2,1)S(1)} %pad_maximum_fusion.8), channel_id=1, source_target_pairs={{0,6},{2,0},{4,2},{6,4},{1,7},{3,1},{5,3},{7,5},{8,14},{10,8},{12,... | collective-permute-start | bytes 1769480 | tf_op jit(solution)/shard_map/x3/ppermute | solution.py:24
  187.9 9.5 %collective-permute-done.32 = bf16[144,2048]{1,0:T(8,128)(2,1)S(1)} collective-permute-done((bf16[144,2048]{1,0:T(8,128)(2,1)S(1)}, bf16[144,2048]{1,0:T(8,128)(2,1)S(1)}, u32[]{:S(2)}, u32[]{:S(2)}) %collective-permute-start.32) | collective-permute-done | bytes 589856 | tf_op jit(solution)/shard_map/x1/ppermute | solution.py:24
  198.4 3.6 %collective-permute-start.35 = (bf16[72,2048]{1,0:T(8,128)(2,1)S(1)}, bf16[72,2048]{1,0:T(8,128)(2,1)S(1)}, u32[]{:S(2)}, u32[]{:S(2)}) collective-permute-start(bf16[72,2048]{1,0:T(8,128)(2,1)S(1)} %get-tuple-element.110), channel_id=1, source_target_pairs={{0,1},{1,0},{2,3},{3,2},{4,5},{5,4},{6,7},{7,6},{8,9},{9,8},{10,11... | collective-permute-start | bytes 884744 | tf_op jit(solution)/shard_map/core/ppermute | solution.py:29
  202.0 8.0 %collective-permute-done.27 = bf16[144,2048]{1,0:T(8,128)(2,1)S(1)} collective-permute-done((bf16[144,2048]{1,0:T(8,128)(2,1)S(1)}, bf16[144,2048]{1,0:T(8,128)(2,1)S(1)}, u32[]{:S(2)}, u32[]{:S(2)}) %collective-permute-start.27) | collective-permute-done | bytes 589856 | tf_op jit(solution)/shard_map/x1/ppermute | solution.py:24
  214.9 2.4 %shard_map.103 = bf16[72,8192]{1,0:T(8,128)(2,1)} custom-call(s32[2]{0:T(128)} %pad_add_fusion.at_ref, bf16[72,2048]{1,0:T(8,128)(2,1)} %get-tuple-element.113.refs_0_, bf16[72,2048]{1,0:T(8,128)(2,1)} %copy-done.12, bf16[72,2048]{1,0:T(8,128)(2,1)} %get-tuple-element.111.refs_2_, bf16[72,2048]{1,0:T(8,128)(2,1)} %copy-done.11), custom_call_target="tpu_custom_call" | custom-call | tf_op jit(solution)/shard_map/pallas_call | solution.py:170
  (214 shorter events, 48.0 us)
Async XLA Ops:
  6.5 69.7 %all-gather.3.cloned.1.call-start = ((), (), s32[]{:S(2)}) async-start(), calls=%async_computation.1 | async-start | bytes 3932160 | tf_op jit(solution)/shard_map/all_gather | solution.py:233
  9.6 153.2 %all-gather.5.cloned.1.call-start = ((), (), s32[]{:S(2)}) async-start(), calls=%async_computation.2 | async-start | bytes 10485760 | tf_op jit(solution)/shard_map/all_gather | solution.py:270
  11.5 16.4 %collective-permute-start.3 = (bf16[72,2048]{1,0:T(8,128)(2,1)S(1)}, bf16[72,2048]{1,0:T(8,128)(2,1)S(1)}, u32[]{:S(2)}, u32[]{:S(2)}) collective-permute-start(bf16[72,2048]{1,0:T(8,128)(2,1)S(1)} %get-tuple-element.53), channel_id=1, source_target_pairs={{0,2},{2,4},{4,6},{6,0},{1,3},{3,5},{5,7},{7,1},{8,10},{10,12},{12... | collective-permute-start | bytes 884744 | tf_op jit(solution)/shard_map/own/x1/ppermute | solution.py:24
  13.5 14.5 %collective-permute-start.4 = (bf16[72,2048]{1,0:T(8,128)(2,1)S(1)}, bf16[72,2048]{1,0:T(8,128)(2,1)S(1)}, u32[]{:S(2)}, u32[]{:S(2)}) collective-permute-start(bf16[72,2048]{1,0:T(8,128)(2,1)S(1)} %get-tuple-element.53), channel_id=1, source_target_pairs={{0,6},{2,0},{4,2},{6,4},{1,7},{3,1},{5,3},{7,5},{8,14},{10,8},{12,... | collective-permute-start | bytes 884744 | tf_op jit(solution)/shard_map/own/x3/ppermute | solution.py:24
  14.8 16.0 %collective-permute-start = (bf16[72,2048]{1,0:T(8,128)(2,1)}, bf16[72,2048]{1,0:T(8,128)(2,1)S(1)}, u32[]{:S(2)}, u32[]{:S(2)}) collective-permute-start(bf16[72,2048]{1,0:T(8,128)(2,1)} %get-tuple-element.91), channel_id=1, source_target_pairs={{0,64},{32,96},{64,0},{96,32},{1,65},{33,97},{65,1},{97,33},{2,66}... | collective-permute-start | bytes 884744 | tf_op jit(solution)/shard_map/exchange/y2/ppermute | solution.py:24
  17.9 14.1 %collective-permute-start.1 = (bf16[72,2048]{1,0:T(8,128)(2,1)}, bf16[72,2048]{1,0:T(8,128)(2,1)S(1)}, u32[]{:S(2)}, u32[]{:S(2)}) collective-permute-start(bf16[72,2048]{1,0:T(8,128)(2,1)} %get-tuple-element.90), channel_id=1, source_target_pairs={{0,32},{32,64},{64,96},{96,0},{1,33},{33,65},{65,97},{97,1},{2,34}... | collective-permute-start | bytes 884744 | tf_op jit(solution)/shard_map/exchange/y1/ppermute | solution.py:24
  23.5 9.0 %collective-permute-start.2 = (bf16[72,2048]{1,0:T(8,128)(2,1)}, bf16[72,2048]{1,0:T(8,128)(2,1)S(1)}, u32[]{:S(2)}, u32[]{:S(2)}) collective-permute-start(bf16[72,2048]{1,0:T(8,128)(2,1)} %get-tuple-element.89), channel_id=1, source_target_pairs={{0,96},{32,0},{64,32},{96,64},{1,97},{33,1},{65,33},{97,65},{2,98}... | collective-permute-start | bytes 884744 | tf_op jit(solution)/shard_map/exchange/y3/ppermute | solution.py:24
  35.0 28.6 %collective-permute-start.10 = (bf16[216,2048]{1,0:T(8,128)(2,1)S(1)}, bf16[216,2048]{1,0:T(8,128)(2,1)S(1)}, u32[]{:S(2)}, u32[]{:S(2)}) collective-permute-start(bf16[216,2048]{1,0:T(8,128)(2,1)S(1)} %pad_maximum_fusion.3.refs_0_), channel_id=1, source_target_pairs={{0,6},{2,0},{4,2},{6,4},{1,7},{3,1},{5,3},{7,5},{8,14},{10,8},{12,... | collective-permute-start | bytes 2654216 | tf_op jit(solution)/shard_map/rest/x3/ppermute | solution.py:24
  36.8 26.8 %collective-permute-start.8 = (bf16[216,2048]{1,0:T(8,128)(2,1)S(1)}, bf16[216,2048]{1,0:T(8,128)(2,1)S(1)}, u32[]{:S(2)}, u32[]{:S(2)}) collective-permute-start(bf16[216,2048]{1,0:T(8,128)(2,1)S(1)} %pad_maximum_fusion.3.refs_0_), channel_id=1, source_target_pairs={{0,2},{2,4},{4,6},{6,0},{1,3},{3,5},{5,7},{7,1},{8,10},{10,12},{12... | collective-permute-start | bytes 2654216 | tf_op jit(solution)/shard_map/rest/x1/ppermute | solution.py:24
  36.8 13.0 %collective-permute-start.12 = (bf16[1024,256]{1,0:T(8,128)(2,1)S(1)}, bf16[1024,256]{1,0:T(8,128)(2,1)S(1)}, u32[]{:S(2)}, u32[]{:S(2)}) collective-permute-start(bf16[1024,256]{1,0:T(8,128)(2,1)S(1)} %pad_maximum_fusion.11), channel_id=1, source_target_pairs={{0,32},{32,64},{64,96},{96,0},{1,33},{33,65},{65,97},{97,1},{2,34}... | collective-permute-start | bytes 1572872 | tf_op jit(solution)/shard_map/w_out/y1/ppermute | solution.py:24
  36.8 24.4 %collective-permute-start.13 = (bf16[1024,256]{1,0:T(8,128)(2,1)S(1)}, bf16[1024,256]{1,0:T(8,128)(2,1)S(1)}, u32[]{:S(2)}, u32[]{:S(2)}) collective-permute-start(bf16[1024,256]{1,0:T(8,128)(2,1)S(1)} %pad_maximum_fusion.11), channel_id=1, source_target_pairs={{0,64},{32,96},{64,0},{96,32},{1,65},{33,97},{65,1},{97,33},{2,66}... | collective-permute-start | bytes 1572872 | tf_op jit(solution)/shard_map/w_out/y2/ppermute | solution.py:24
  39.4 22.7 %collective-permute-start.14 = (bf16[1024,256]{1,0:T(8,128)(2,1)S(1)}, bf16[1024,256]{1,0:T(8,128)(2,1)S(1)}, u32[]{:S(2)}, u32[]{:S(2)}) collective-permute-start(bf16[1024,256]{1,0:T(8,128)(2,1)S(1)} %pad_maximum_fusion.11), channel_id=1, source_target_pairs={{0,96},{32,0},{64,32},{96,64},{1,97},{33,1},{65,33},{97,65},{2,98}... | collective-permute-start | bytes 1572872 | tf_op jit(solution)/shard_map/w_out/y3/ppermute | solution.py:24
  63.7 17.2 %collective-permute-start.15 = (bf16[216,2048]{1,0:T(8,128)(2,1)S(1)}, bf16[216,2048]{1,0:T(8,128)(2,1)}, u32[]{:S(2)}, u32[]{:S(2)}) collective-permute-start(bf16[216,2048]{1,0:T(8,128)(2,1)S(1)} %pad_maximum_fusion.3.refs_0_), channel_id=1, source_target_pairs={{0,1},{1,0},{2,3},{3,2},{4,5},{5,4},{6,7},{7,6},{8,9},{9,8},{10,11... | collective-permute-start | bytes 2654216 | tf_op jit(solution)/shard_map/core/ppermute | solution.py:29
  66.0 14.9 %collective-permute-start.16 = (bf16[216,2048]{1,0:T(8,128)(2,1)S(1)}, bf16[216,2048]{1,0:T(8,128)(2,1)}, u32[]{:S(2)}, u32[]{:S(2)}) collective-permute-start(bf16[216,2048]{1,0:T(8,128)(2,1)S(1)} %collective-permute-done.8.refs_1_), channel_id=1, source_target_pairs={{0,1},{1,0},{2,3},{3,2},{4,5},{5,4},{6,7},{7,6},{8,9},{9,8},{10,11... | collective-permute-start | bytes 2654216 | tf_op jit(solution)/shard_map/rest/core/ppermute | solution.py:29
  66.1 14.8 %collective-permute-start.17 = (bf16[216,2048]{1,0:T(8,128)(2,1)S(1)}, bf16[216,2048]{1,0:T(8,128)(2,1)}, u32[]{:S(2)}, u32[]{:S(2)}) collective-permute-start(bf16[216,2048]{1,0:T(8,128)(2,1)S(1)} %collective-permute-done.10.refs_2_), channel_id=1, source_target_pairs={{0,1},{1,0},{2,3},{3,2},{4,5},{5,4},{6,7},{7,6},{8,9},{9,8},{10,11... | collective-permute-start | bytes 2654216 | tf_op jit(solution)/shard_map/rest/core/ppermute | solution.py:29
  68.2 17.0 %collective-permute-start.11 = (bf16[216,1024]{1,0:T(8,128)(2,1)}, bf16[216,1024]{1,0:T(8,128)(2,1)}, u32[]{:S(2)}, u32[]{:S(2)}) collective-permute-start(bf16[216,1024]{1,0:T(8,128)(2,1)} %slice.251), channel_id=1, source_target_pairs={{0,6},{2,0},{4,2},{6,4},{1,7},{3,1},{5,3},{7,5},{8,14},{10,8},{12,... | collective-permute-start | bytes 1327112 | tf_op jit(solution)/shard_map/rest/x3/ppermute | solution.py:24
  71.7 13.6 %collective-permute-start.9 = (bf16[216,1024]{1,0:T(8,128)(2,1)}, bf16[216,1024]{1,0:T(8,128)(2,1)}, u32[]{:S(2)}, u32[]{:S(2)}) collective-permute-start(bf16[216,1024]{1,0:T(8,128)(2,1)} %slice.250), channel_id=1, source_target_pairs={{0,2},{2,4},{4,6},{6,0},{1,3},{3,5},{5,7},{7,1},{8,10},{10,12},{12... | collective-permute-start | bytes 1327112 | tf_op jit(solution)/shard_map/rest/x1/ppermute | solution.py:24
  86.0 21.0 %collective-permute-start.18 = (bf16[288,2048]{1,0:T(8,128)(2,1)S(1)}, bf16[288,2048]{1,0:T(8,128)(2,1)S(1)}, u32[]{:S(2)}, u32[]{:S(2)}) collective-permute-start(bf16[288,2048]{1,0:T(8,128)(2,1)S(1)} %pad_maximum_fusion.2), channel_id=1, source_target_pairs={{0,1},{1,0},{2,3},{3,2},{4,5},{5,4},{6,7},{7,6},{8,9},{9,8},{10,11... | collective-permute-start | bytes 3538952 | tf_op jit(solution)/shard_map/own/core/ppermute | solution.py:29
  90.0 11.9 %collective-permute-start.23 = (bf16[576,384]{1,0:T(8,128)(2,1)S(1)}, bf16[576,384]{1,0:T(8,128)(2,1)S(1)}, u32[]{:S(2)}, u32[]{:S(2)}) collective-permute-start(bf16[576,384]{1,0:T(8,128)(2,1)S(1)} %get-tuple-element.92), channel_id=1, source_target_pairs={{0,96},{32,0},{64,32},{96,64},{1,97},{33,1},{65,33},{97,65},{2,98}... | collective-permute-start | bytes 1327112 | tf_op jit(solution)/shard_map/y3/ppermute | solution.py:24
  92.1 13.3 %collective-permute-start.21 = (bf16[576,384]{1,0:T(8,128)(2,1)S(1)}, bf16[576,384]{1,0:T(8,128)(2,1)S(1)}, u32[]{:S(2)}, u32[]{:S(2)}) collective-permute-start(bf16[576,384]{1,0:T(8,128)(2,1)S(1)} %get-tuple-element.93), channel_id=1, source_target_pairs={{0,32},{32,64},{64,96},{96,0},{1,33},{33,65},{65,97},{97,1},{2,34}... | collective-permute-start | bytes 1327112 | tf_op jit(solution)/shard_map/y1/ppermute | solution.py:24
  102.1 21.6 %collective-permute-start.24 = (bf16[576,768]{1,0:T(8,128)(2,1)S(1)}, bf16[576,768]{1,0:T(8,128)(2,1)S(1)}, u32[]{:S(2)}, u32[]{:S(2)}) collective-permute-start(bf16[576,768]{1,0:T(8,128)(2,1)S(1)} %pad_maximum_fusion.5), channel_id=1, source_target_pairs={{0,96},{32,0},{64,32},{96,64},{1,97},{33,1},{65,33},{97,65},{2,98}... | collective-permute-start | bytes 2654216 | tf_op jit(solution)/shard_map/y3/ppermute | solution.py:24
  105.6 21.7 %collective-permute-start.22 = (bf16[576,768]{1,0:T(8,128)(2,1)S(1)}, bf16[576,768]{1,0:T(8,128)(2,1)S(1)}, u32[]{:S(2)}, u32[]{:S(2)}) collective-permute-start(bf16[576,768]{1,0:T(8,128)(2,1)S(1)} %pad_maximum_fusion.4), channel_id=1, source_target_pairs={{0,32},{32,64},{64,96},{96,0},{1,33},{33,65},{65,97},{97,1},{2,34}... | collective-permute-start | bytes 2654216 | tf_op jit(solution)/shard_map/y1/ppermute | solution.py:24
  134.7 21.3 %all-to-all-start = ((bf16[16,72,512]{2,1,0:T(8,128)(2,1)}), bf16[16,72,512]{2,1,0:T(8,128)(2,1)S(1)}, u32[]{:S(2)}, u32[]{:S(2)}) async-start(bf16[16,72,512]{2,1,0:T(8,128)(2,1)} %bitcast.16), calls=%async_computation | async-start | bytes 2359296 | tf_op jit(solution)/shard_map/all_to_all | solution.py:330
  167.9 10.8 %collective-permute-start.31 = (bf16[144,1024]{1,0:T(8,128)(2,1)S(1)}, bf16[144,1024]{1,0:T(8,128)(2,1)S(1)}, u32[]{:S(2)}, u32[]{:S(2)}) collective-permute-start(bf16[144,1024]{1,0:T(8,128)(2,1)S(1)} %get-tuple-element.78), channel_id=1, source_target_pairs={{0,2},{2,4},{4,6},{6,0},{1,3},{3,5},{5,7},{7,1},{8,10},{10,12},{12... | collective-permute-start | bytes 884744 | tf_op jit(solution)/shard_map/x1/ppermute | solution.py:24
  169.2 9.5 %collective-permute-start.33 = (bf16[144,1024]{1,0:T(8,128)(2,1)S(1)}, bf16[144,1024]{1,0:T(8,128)(2,1)S(1)}, u32[]{:S(2)}, u32[]{:S(2)}) collective-permute-start(bf16[144,1024]{1,0:T(8,128)(2,1)S(1)} %get-tuple-element.79), channel_id=1, source_target_pairs={{0,6},{2,0},{4,2},{6,4},{1,7},{3,1},{5,3},{7,5},{8,14},{10,8},{12,... | collective-permute-start | bytes 884744 | tf_op jit(solution)/shard_map/x3/ppermute | solution.py:24
  176.0 8.7 %collective-permute-start.26 = (bf16[144,1024]{1,0:T(8,128)(2,1)S(1)}, bf16[144,1024]{1,0:T(8,128)(2,1)S(1)}, u32[]{:S(2)}, u32[]{:S(2)}) collective-permute-start(bf16[144,1024]{1,0:T(8,128)(2,1)S(1)} %get-tuple-element.84), channel_id=1, source_target_pairs={{0,2},{2,4},{4,6},{6,0},{1,3},{3,5},{5,7},{7,1},{8,10},{10,12},{12... | collective-permute-start | bytes 884744 | tf_op jit(solution)/shard_map/x1/ppermute | solution.py:24
  176.1 8.6 %collective-permute-start.28 = (bf16[144,1024]{1,0:T(8,128)(2,1)S(1)}, bf16[144,1024]{1,0:T(8,128)(2,1)S(1)}, u32[]{:S(2)}, u32[]{:S(2)}) collective-permute-start(bf16[144,1024]{1,0:T(8,128)(2,1)S(1)} %get-tuple-element.85), channel_id=1, source_target_pairs={{0,6},{2,0},{4,2},{6,4},{1,7},{3,1},{5,3},{7,5},{8,14},{10,8},{12,... | collective-permute-start | bytes 884744 | tf_op jit(solution)/shard_map/x3/ppermute | solution.py:24
  179.0 18.3 %collective-permute-start.32 = (bf16[144,2048]{1,0:T(8,128)(2,1)S(1)}, bf16[144,2048]{1,0:T(8,128)(2,1)S(1)}, u32[]{:S(2)}, u32[]{:S(2)}) collective-permute-start(bf16[144,2048]{1,0:T(8,128)(2,1)S(1)} %pad_maximum_fusion.9), channel_id=1, source_target_pairs={{0,2},{2,4},{4,6},{6,0},{1,3},{3,5},{5,7},{7,1},{8,10},{10,12},{12... | collective-permute-start | bytes 1769480 | tf_op jit(solution)/shard_map/x1/ppermute | solution.py:24
  179.1 18.2 %collective-permute-start.34 = (bf16[144,2048]{1,0:T(8,128)(2,1)S(1)}, bf16[144,2048]{1,0:T(8,128)(2,1)S(1)}, u32[]{:S(2)}, u32[]{:S(2)}) collective-permute-start(bf16[144,2048]{1,0:T(8,128)(2,1)S(1)} %pad_maximum_fusion.10), channel_id=1, source_target_pairs={{0,6},{2,0},{4,2},{6,4},{1,7},{3,1},{5,3},{7,5},{8,14},{10,8},{12,... | collective-permute-start | bytes 1769480 | tf_op jit(solution)/shard_map/x3/ppermute | solution.py:24
  185.0 25.0 %collective-permute-start.27 = (bf16[144,2048]{1,0:T(8,128)(2,1)S(1)}, bf16[144,2048]{1,0:T(8,128)(2,1)S(1)}, u32[]{:S(2)}, u32[]{:S(2)}) collective-permute-start(bf16[144,2048]{1,0:T(8,128)(2,1)S(1)} %pad_maximum_fusion.7), channel_id=1, source_target_pairs={{0,2},{2,4},{4,6},{6,0},{1,3},{3,5},{5,7},{7,1},{8,10},{10,12},{12... | collective-permute-start | bytes 1769480 | tf_op jit(solution)/shard_map/x1/ppermute | solution.py:24
  185.1 24.9 %collective-permute-start.29 = (bf16[144,2048]{1,0:T(8,128)(2,1)S(1)}, bf16[144,2048]{1,0:T(8,128)(2,1)S(1)}, u32[]{:S(2)}, u32[]{:S(2)}) collective-permute-start(bf16[144,2048]{1,0:T(8,128)(2,1)S(1)} %pad_maximum_fusion.8), channel_id=1, source_target_pairs={{0,6},{2,0},{4,2},{6,4},{1,7},{3,1},{5,3},{7,5},{8,14},{10,8},{12,... | collective-permute-start | bytes 1769480 | tf_op jit(solution)/shard_map/x3/ppermute | solution.py:24
  198.4 15.3 %collective-permute-start.35 = (bf16[72,2048]{1,0:T(8,128)(2,1)S(1)}, bf16[72,2048]{1,0:T(8,128)(2,1)S(1)}, u32[]{:S(2)}, u32[]{:S(2)}) collective-permute-start(bf16[72,2048]{1,0:T(8,128)(2,1)S(1)} %get-tuple-element.110), channel_id=1, source_target_pairs={{0,1},{1,0},{2,3},{3,2},{4,5},{5,4},{6,7},{7,6},{8,9},{9,8},{10,11... | collective-permute-start | bytes 884744 | tf_op jit(solution)/shard_map/core/ppermute | solution.py:29
  (38 other events, 235.3 us)
Sparse Core Ops, SparseCore 0:
  9.8 42.9 all-gather.2
  63.8 98.9 all-gather.4

commit v2 on v1

--- a/solution.py
+++ b/solution.py
@@ -261,17 +261,17 @@
 
     rest_other = swap(rest)
     with jax.named_scope("w_out"):
-        w_near = jnp.stack([w_both, hop(w_both, "y", 1), hop(w_both, "y", 2), hop(w_both, "y", 3)])
+        w_near = [w_both] + [hop(w_both, "y", i) for i in range(1, ny)]
 
     with jax.named_scope("rest"):
         left, right = hop(rest, "x", 1), hop(rest, "x", -1)
         low, high = hop(left[:, :half], "x", 1), hop(right[:, half:], "x", -1)
-    w_near, left, right = after(w_near, left, right)
-    w_out = lax.all_gather(w_near, "z", axis=0, tiled=True)
+    w_near, low, high, left_in, right_in = after(w_near, low, high, left, right)
+    w_out = lax.all_gather(jnp.stack(w_near), "z", axis=0, tiled=True)
 
     with jax.named_scope("rest"):
         near = [rest, left, right]
-        near_sums = [multiply([[t] for t in side], w_in) for side in (near, [rest_other, swap(left), swap(right)])]
+        near_sums = [multiply([[t] for t in side], w_in) for side in (near, [rest_other, swap(left_in), swap(right_in)])]
         (low, high), near_sums, mine = after(
             (low, high), near_sums, (pack_0, left_0, low_0, high_0, right_0)
         )

time: 225 us -> 230 us (1.022)
  waiting for transfers between devices: 93.6 us -> 98.9 us
  local copies, waits for them, and re-layouts: 10.4 us -> 7.66 us
  starting transfers between devices: 56.8 us -> 59.4 us
    all_gather x1, waiting for transfers between devices: 0.07 us -> 5.4 us  [shards(): w_out = lax.all_gather(jnp.stack(w_near), 'z', axis=0, tiled=True)]
    unnamed x77 -> x79, local copies, waits for them, and re-layouts: 5.21 us -> 4.13 us
  transfers between devices with their start and end apart: 39 -> 39, of which waited for: 16 -> 16; matrix products, arithmetic and copies ran while one was open for 10% -> 9% of each run, Pallas kernels for 10% -> 10%
where the time goes in v2:
time: 230 us; the launch traced here: 229 us
  waiting for transfers between devices  98.9 us (43%)
  starting transfers between devices  59.4 us (26%)
  Pallas kernels  29.3 us (13%)
  other arithmetic  16.5 us (7%)
  between operations  14.5 us (6%)
  local copies, waits for them, and re-layouts  7.66 us (3%)
  matrix products  3.14 us (1%)
    ppermute x26, waiting for transfers between devices, hop(): return lax.ppermute(v, axis, ring(lax.axis_size(axis), step))  75.5 us
    ppermute x26, starting transfers between devices, hop(): return lax.ppermute(v, axis, ring(lax.axis_size(axis), step))  36.5 us
    ppermute x10, starting transfers between devices, swap(): return lax.ppermute(v, 'c', [(0, 1), (1, 0)])  17.3 us
    all_to_all x1, waiting for transfers between devices, shards(): got = lax.all_to_all(sent, DP, split_axis=0, concat_axis=0, tiled=True)  15.7 us
    pallas_call x2, Pallas kernels, project_out(): pl.pallas_call(project_out_kernel, out_shape=jax.ShapeDtypeStruct((rows,...  9.96 us
    pallas_call x4, Pallas kernels, multiply(): pl.pallas_call(functools.partial(multiply_kernel, [len(pieces) for pieces...  9.56 us
    pallas_call x1, Pallas kernels, attend(): pl.pallas_call(functools.partial(attend_kernel, here, heads), out_shape=j...  7.38 us
    all_to_all x1, starting transfers between devices, shards(): got = lax.all_to_all(sent, DP, split_axis=0, concat_axis=0, tiled=True)  5.53 us
  transfers between devices with their start and end apart: 39, of which 16 were waited for; matrix products, arithmetic and copies ran while one was open for 9% of the time, Pallas kernels for 10%

profile of v2, /device:TPU:1, one launch (start us, length us, event | category | flops | bytes accessed | tf_op | source)
XLA Modules:
  0.0 229.4 jit_solution(10318529395009725964)
XLA Ops:
  11.2 2.0 collective-permute-start.3
  14.5 3.1 %collective-permute-start = (bf16[72,2048]{1,0:T(8,128)(2,1)}, bf16[72,2048]{1,0:T(8,128)(2,1)S(1)}, u32[]{:S(2)}, u32[]{:S(2)}) collective-permute-start(bf16[72,2048]{1,0:T(8,128)(2,1)} %get-tuple-element.101), channel_id=1, source_target_pairs={{0,64},{32,96},{64,0},{96,32},{1,65},{33,97},{65,1},{97,33},{2,66}... | collective-permute-start | bytes 884744 | tf_op jit(solution)/shard_map/exchange/y2/ppermute | solution.py:24
  23.4 2.3 %collective-permute-start.2 = (bf16[72,2048]{1,0:T(8,128)(2,1)S(1)}, bf16[72,2048]{1,0:T(8,128)(2,1)S(1)}, u32[]{:S(2)}, u32[]{:S(2)}) collective-permute-start(bf16[72,2048]{1,0:T(8,128)(2,1)S(1)} %get-tuple-element.99), channel_id=1, source_target_pairs={{0,96},{32,0},{64,32},{96,64},{1,97},{33,1},{65,33},{97,65},{2,98}... | collective-permute-start | bytes 884744 | tf_op jit(solution)/shard_map/exchange/y3/ppermute | solution.py:24
  27.9 2.7 %collective-permute-start.6 = (bf16[72,1024]{1,0:T(8,128)(2,1)S(1)}, bf16[72,1024]{1,0:T(8,128)(2,1)S(1)}, u32[]{:S(2)}, u32[]{:S(2)}) collective-permute-start(bf16[72,1024]{1,0:T(8,128)(2,1)S(1)} %slice.249), channel_id=1, source_target_pairs={{0,6},{2,0},{4,2},{6,4},{1,7},{3,1},{5,3},{7,5},{8,14},{10,8},{12,... | collective-permute-start | bytes 442376 | tf_op jit(solution)/shard_map/own/x3/ppermute | solution.py:24
  34.3 2.7 %collective-permute-start.13 = (bf16[216,2048]{1,0:T(8,128)(2,1)S(1)}, bf16[216,2048]{1,0:T(8,128)(2,1)S(1)}, u32[]{:S(2)}, u32[]{:S(2)}) collective-permute-start(bf16[216,2048]{1,0:T(8,128)(2,1)S(1)} %pad_maximum_fusion.3.refs_0_), channel_id=1, source_target_pairs={{0,6},{2,0},{4,2},{6,4},{1,7},{3,1},{5,3},{7,5},{8,14},{10,8},{12,... | collective-permute-start | bytes 2654216 | tf_op jit(solution)/shard_map/rest/x3/ppermute | solution.py:24
  39.7 16.0 %collective-permute-done.11.refs_1_ = bf16[216,2048]{1,0:T(8,128)(2,1)S(1)} collective-permute-done((bf16[216,2048]{1,0:T(8,128)(2,1)S(1)}, bf16[216,2048]{1,0:T(8,128)(2,1)S(1)}, u32[]{:S(2)}, u32[]{:S(2)}) %collective-permute-start.11) | collective-permute-done | bytes 884768 | tf_op jit(solution)/shard_map/rest/x1/ppermute | solution.py:24
  55.8 2.7 %collective-permute-start.14 = (bf16[216,1024]{1,0:T(8,128)(2,1)S(1)}, bf16[216,1024]{1,0:T(8,128)(2,1)}, u32[]{:S(2)}, u32[]{:S(2)}) collective-permute-start(bf16[216,1024]{1,0:T(8,128)(2,1)S(1)} %slice.251), channel_id=1, source_target_pairs={{0,6},{2,0},{4,2},{6,4},{1,7},{3,1},{5,3},{7,5},{8,14},{10,8},{12,... | collective-permute-start | bytes 1327112 | tf_op jit(solution)/shard_map/rest/x3/ppermute | solution.py:24
  58.6 3.0 %collective-permute-done.9 = bf16[1024,256]{1,0:T(8,128)(2,1)S(1)} collective-permute-done((bf16[1024,256]{1,0:T(8,128)(2,1)S(1)}, bf16[1024,256]{1,0:T(8,128)(2,1)S(1)}, u32[]{:S(2)}, u32[]{:S(2)}) %collective-permute-start.9) | collective-permute-done | bytes 524320 | tf_op jit(solution)/shard_map/w_out/y2/ppermute | solution.py:24
  61.5 5.2 %collective-permute-done.12.refs_0_ = bf16[216,1024]{1,0:T(8,128)(2,1)S(1)} collective-permute-done((bf16[216,1024]{1,0:T(8,128)(2,1)S(1)}, bf16[216,1024]{1,0:T(8,128)(2,1)S(1)}, u32[]{:S(2)}, u32[]{:S(2)}) %collective-permute-start.12) | collective-permute-done | bytes 442400 | tf_op jit(solution)/shard_map/rest/x1/ppermute | solution.py:24
  68.4 2.9 %collective-permute-start.15 = (bf16[216,2048]{1,0:T(8,128)(2,1)S(1)}, bf16[216,2048]{1,0:T(8,128)(2,1)}, u32[]{:S(2)}, u32[]{:S(2)}) collective-permute-start(bf16[216,2048]{1,0:T(8,128)(2,1)S(1)} %pad_maximum_fusion.3.refs_0_), channel_id=1, source_target_pairs={{0,1},{1,0},{2,3},{3,2},{4,5},{5,4},{6,7},{7,6},{8,9},{9,8},{10,11... | collective-permute-start | bytes 2654216 | tf_op jit(solution)/shard_map/core/ppermute | solution.py:29
  79.1 2.3 %rest.4 = (f32[216,768]{1,0:T(8,128)S(1)}, f32[216,768]{1,0:T(8,128)S(1)}, f32[216,768]{1,0:T(8,128)S(1)}) custom-call(bf16[2048,768]{1,0:T(8,128)(2,1)S(1)} %copy-done, bf16[216,2048]{1,0:T(8,128)(2,1)S(1)} %pad_maximum_fusion.3.refs_0_, bf16[216,2048]{1,0:T(8,128)(2,1)S(1)} %collective-permute-done.11.refs_1_, ...), custom_call_target="tpu_custom_call" | custom-call | flops 1048576 | bytes 4096 | tf_op jit(solution)/shard_map/rest/pallas_call | solution.py:120
  81.5 4.5 %rest.5 = (f32[216,768]{1,0:T(8,128)S(1)}, f32[216,768]{1,0:T(8,128)S(1)}, f32[216,768]{1,0:T(8,128)S(1)}) custom-call(bf16[2048,768]{1,0:T(8,128)(2,1)S(1)} %copy-done, bf16[216,2048]{1,0:T(8,128)(2,1)} %collective-permute-done.15.refs_0_, bf16[216,2048]{1,0:T(8,128)(2,1)} %collective-permute-done.16.refs_1_, bf16[216,2048]{1,0:T(8,128)(2,1)} %collective-permute-done.17.refs_2_), custom_call_target="tpu_custom_call" | custom-call | flops 1048576 | bytes 4096 | tf_op jit(solution)/shard_map/rest/pallas_call | solution.py:120
  92.3 9.4 %collective-permute-done.23 = bf16[576,384]{1,0:T(8,128)(2,1)S(1)} collective-permute-done((bf16[576,384]{1,0:T(8,128)(2,1)S(1)}, bf16[576,384]{1,0:T(8,128)(2,1)S(1)}, u32[]{:S(2)}, u32[]{:S(2)}) %collective-permute-start.23) | collective-permute-done | bytes 442400 | tf_op jit(solution)/shard_map/y3/ppermute | solution.py:24
  101.9 3.1 %collective-permute-start.24 = (bf16[576,768]{1,0:T(8,128)(2,1)S(1)}, bf16[576,768]{1,0:T(8,128)(2,1)S(1)}, u32[]{:S(2)}, u32[]{:S(2)}) collective-permute-start(bf16[576,768]{1,0:T(8,128)(2,1)S(1)} %pad_maximum_fusion.5), channel_id=1, source_target_pairs={{0,96},{32,0},{64,32},{96,64},{1,97},{33,1},{65,33},{97,65},{2,98}... | collective-permute-start | bytes 2654216 | tf_op jit(solution)/shard_map/y3/ppermute | solution.py:24
  107.9 15.0 %collective-permute-done.24.p_ref = bf16[576,768]{1,0:T(8,128)(2,1)S(1)} collective-permute-done((bf16[576,768]{1,0:T(8,128)(2,1)S(1)}, bf16[576,768]{1,0:T(8,128)(2,1)S(1)}, u32[]{:S(2)}, u32[]{:S(2)}) %collective-permute-start.24) | collective-permute-done | bytes 884768 | tf_op jit(solution)/shard_map/y3/ppermute | solution.py:24
  122.8 3.7 %collective-permute-done.22.m_ref = bf16[576,768]{1,0:T(8,128)(2,1)S(1)} collective-permute-done((bf16[576,768]{1,0:T(8,128)(2,1)S(1)}, bf16[576,768]{1,0:T(8,128)(2,1)S(1)}, u32[]{:S(2)}, u32[]{:S(2)}) %collective-permute-start.22) | collective-permute-done | bytes 884768 | tf_op jit(solution)/shard_map/y1/ppermute | solution.py:24
  126.5 7.4 %shard_map.100 = bf16[1152,512]{1,0:T(8,128)(2,1)} custom-call(s32[1]{0:T(128)} %bitcast.core_ref, f32[576,768]{1,0:T(8,128)S(1)} %pad_maximum_fusion.1.sum_ref, bf16[576,768]{1,0:T(8,128)(2,1)S(1)} %collective-permute-done.22.m_ref, bf16[576,768]{1,0:T(8,128)(2,1)S(1)} %collective-permute-done.24.p_ref, f32[1,768]{1,0:T(1,128)S(1)} %broadcast_in_dim.14.bias_ref, ...), custom_call_target="tpu_custom_call" | custom-call | flops 1073741824 | bytes 8388608 | tf_op jit(solution)/shard_map/pallas_call | solution.py:87
  133.9 5.5 %all-to-all-start = ((bf16[16,72,512]{2,1,0:T(8,128)(2,1)}), bf16[16,72,512]{2,1,0:T(8,128)(2,1)S(1)}, u32[]{:S(2)}, u32[]{:S(2)}) async-start(bf16[16,72,512]{2,1,0:T(8,128)(2,1)} %bitcast.12), calls=%async_computation | async-start | bytes 2359296 | tf_op jit(solution)/shard_map/all_to_all | solution.py:330
  139.5 15.7 %all-to-all-done = bf16[16,72,512]{2,1,0:T(8,128)(2,1)S(1)} async-done(((bf16[16,72,512]{2,1,0:T(8,128)(2,1)}), bf16[16,72,512]{2,1,0:T(8,128)(2,1)S(1)}, u32[]{:S(2)}, u32[]{:S(2)}) %all-to-all-start) | async-done | bytes 1179680 | tf_op jit(solution)/shard_map/all_to_all | solution.py:330
  156.2 5.1 %collective-permute-start.25 = (bf16[576,512]{1,0:T(8,128)(2,1)S(1)}, bf16[576,512]{1,0:T(8,128)(2,1)S(1)}, u32[]{:S(2)}, u32[]{:S(2)}) collective-permute-start(bf16[576,512]{1,0:T(8,128)(2,1)S(1)} %fusion.5.mine_ref), channel_id=1, source_target_pairs={{0,1},{1,0},{2,3},{3,2},{4,5},{5,4},{6,7},{7,6},{8,9},{9,8},{10,11... | collective-permute-start | bytes 1769480 | tf_op jit(solution)/shard_map/core/ppermute | solution.py:29
  162.9 5.4 %all-gather.5.cloned.1.call-done.w_ref = bf16[16,1024,256]{2,1,0:T(8,128)(2,1)} async-done(((bf16[4,1024,256]{2,1,0:T(8,128)(2,1)}), bf16[16,1024,256]{2,1,0:T(8,128)(2,1)}) %all-gather.5.cloned.1.call-update) | async-done | bytes 8388624 | tf_op jit(solution)/shard_map/all_gather | solution.py:270
  168.3 5.0 %shard_map.102 = bf16[576,2048]{1,0:T(8,128)(2,1)S(1)} custom-call(bf16[576,512]{1,0:T(8,128)(2,1)S(1)} %fusion.5.mine_ref, bf16[576,512]{1,0:T(8,128)(2,1)S(1)} %collective-permute-done.25.theirs_ref, bf16[16,1024,256]{2,1,0:T(8,128)(2,1)} %all-gather.5.cloned.1.call-done.w_ref), custom_call_target="tpu_custom_call" | custom-call | flops 2415919104 | bytes 8388608 | tf_op jit(solution)/shard_map/pallas_call | solution.py:141
  176.2 5.0 %shard_map.101 = bf16[576,2048]{1,0:T(8,128)(2,1)S(1)} custom-call(bf16[576,512]{1,0:T(8,128)(2,1)S(1)} %fusion.5.mine_ref, bf16[576,512]{1,0:T(8,128)(2,1)S(1)} %collective-permute-done.25.theirs_ref, bf16[16,1024,256]{2,1,0:T(8,128)(2,1)} %all-gather.5.cloned.1.call-done.w_ref), custom_call_target="tpu_custom_call" | custom-call | flops 2415919104 | bytes 8388608 | tf_op jit(solution)/shard_map/pallas_call | solution.py:141
  181.3 2.7 %collective-permute-start.28 = (bf16[144,1024]{1,0:T(8,128)(2,1)S(1)}, bf16[144,1024]{1,0:T(8,128)(2,1)S(1)}, u32[]{:S(2)}, u32[]{:S(2)}) collective-permute-start(bf16[144,1024]{1,0:T(8,128)(2,1)S(1)} %get-tuple-element.95), channel_id=1, source_target_pairs={{0,6},{2,0},{4,2},{6,4},{1,7},{3,1},{5,3},{7,5},{8,14},{10,8},{12,... | collective-permute-start | bytes 884744 | tf_op jit(solution)/shard_map/x3/ppermute | solution.py:24
  184.4 2.7 %collective-permute-start.34 = (bf16[144,2048]{1,0:T(8,128)(2,1)S(1)}, bf16[144,2048]{1,0:T(8,128)(2,1)S(1)}, u32[]{:S(2)}, u32[]{:S(2)}) collective-permute-start(bf16[144,2048]{1,0:T(8,128)(2,1)S(1)} %pad_maximum_fusion.10), channel_id=1, source_target_pairs={{0,6},{2,0},{4,2},{6,4},{1,7},{3,1},{5,3},{7,5},{8,14},{10,8},{12,... | collective-permute-start | bytes 1769480 | tf_op jit(solution)/shard_map/x3/ppermute | solution.py:24
  187.1 2.6 %collective-permute-done.26 = bf16[144,1024]{1,0:T(8,128)(2,1)S(1)} collective-permute-done((bf16[144,1024]{1,0:T(8,128)(2,1)S(1)}, bf16[144,1024]{1,0:T(8,128)(2,1)S(1)}, u32[]{:S(2)}, u32[]{:S(2)}) %collective-permute-start.26) | collective-permute-done | bytes 294944 | tf_op jit(solution)/shard_map/x1/ppermute | solution.py:24
  190.2 2.7 %collective-permute-start.29 = (bf16[144,2048]{1,0:T(8,128)(2,1)S(1)}, bf16[144,2048]{1,0:T(8,128)(2,1)S(1)}, u32[]{:S(2)}, u32[]{:S(2)}) collective-permute-start(bf16[144,2048]{1,0:T(8,128)(2,1)S(1)} %pad_maximum_fusion.8), channel_id=1, source_target_pairs={{0,6},{2,0},{4,2},{6,4},{1,7},{3,1},{5,3},{7,5},{8,14},{10,8},{12,... | collective-permute-start | bytes 1769480 | tf_op jit(solution)/shard_map/x3/ppermute | solution.py:24
  192.9 9.5 %collective-permute-done.32 = bf16[144,2048]{1,0:T(8,128)(2,1)S(1)} collective-permute-done((bf16[144,2048]{1,0:T(8,128)(2,1)S(1)}, bf16[144,2048]{1,0:T(8,128)(2,1)S(1)}, u32[]{:S(2)}, u32[]{:S(2)}) %collective-permute-start.32) | collective-permute-done | bytes 589856 | tf_op jit(solution)/shard_map/x1/ppermute | solution.py:24
  203.4 4.0 %collective-permute-start.35 = (bf16[72,2048]{1,0:T(8,128)(2,1)S(1)}, bf16[72,2048]{1,0:T(8,128)(2,1)S(1)}, u32[]{:S(2)}, u32[]{:S(2)}) collective-permute-start(bf16[72,2048]{1,0:T(8,128)(2,1)S(1)} %get-tuple-element.120), channel_id=1, source_target_pairs={{0,1},{1,0},{2,3},{3,2},{4,5},{5,4},{6,7},{7,6},{8,9},{9,8},{10,11... | collective-permute-start | bytes 884744 | tf_op jit(solution)/shard_map/core/ppermute | solution.py:29
  207.4 7.6 %collective-permute-done.27 = bf16[144,2048]{1,0:T(8,128)(2,1)S(1)} collective-permute-done((bf16[144,2048]{1,0:T(8,128)(2,1)S(1)}, bf16[144,2048]{1,0:T(8,128)(2,1)S(1)}, u32[]{:S(2)}, u32[]{:S(2)}) %collective-permute-start.27) | collective-permute-done | bytes 589856 | tf_op jit(solution)/shard_map/x1/ppermute | solution.py:24
  216.1 2.2 collective-permute-start.30
  220.2 2.4 %shard_map.103 = bf16[72,8192]{1,0:T(8,128)(2,1)} custom-call(s32[2]{0:T(128)} %pad_add_fusion.at_ref, bf16[72,2048]{1,0:T(8,128)(2,1)} %get-tuple-element.123.refs_0_, bf16[72,2048]{1,0:T(8,128)(2,1)} %copy-done.14, bf16[72,2048]{1,0:T(8,128)(2,1)} %get-tuple-element.121.refs_2_, bf16[72,2048]{1,0:T(8,128)(2,1)} %copy-done.13), custom_call_target="tpu_custom_call" | custom-call | tf_op jit(solution)/shard_map/pallas_call | solution.py:170
  (216 shorter events, 48.9 us)
Async XLA Ops:
  6.5 70.7 %all-gather.3.cloned.1.call-start = ((), (), s32[]{:S(2)}) async-start(), calls=%async_computation.1 | async-start | bytes 3932160 | tf_op jit(solution)/shard_map/all_gather | solution.py:233
  11.2 16.5 %collective-permute-start.3 = (bf16[72,2048]{1,0:T(8,128)(2,1)S(1)}, bf16[72,2048]{1,0:T(8,128)(2,1)S(1)}, u32[]{:S(2)}, u32[]{:S(2)}) collective-permute-start(bf16[72,2048]{1,0:T(8,128)(2,1)S(1)} %get-tuple-element.60), channel_id=1, source_target_pairs={{0,2},{2,4},{4,6},{6,0},{1,3},{3,5},{5,7},{7,1},{8,10},{10,12},{12... | collective-permute-start | bytes 884744 | tf_op jit(solution)/shard_map/own/x1/ppermute | solution.py:24
  13.3 14.6 %collective-permute-start.4 = (bf16[72,2048]{1,0:T(8,128)(2,1)S(1)}, bf16[72,2048]{1,0:T(8,128)(2,1)S(1)}, u32[]{:S(2)}, u32[]{:S(2)}) collective-permute-start(bf16[72,2048]{1,0:T(8,128)(2,1)S(1)} %get-tuple-element.60), channel_id=1, source_target_pairs={{0,6},{2,0},{4,2},{6,4},{1,7},{3,1},{5,3},{7,5},{8,14},{10,8},{12,... | collective-permute-start | bytes 884744 | tf_op jit(solution)/shard_map/own/x3/ppermute | solution.py:24
  14.5 16.1 %collective-permute-start = (bf16[72,2048]{1,0:T(8,128)(2,1)}, bf16[72,2048]{1,0:T(8,128)(2,1)S(1)}, u32[]{:S(2)}, u32[]{:S(2)}) collective-permute-start(bf16[72,2048]{1,0:T(8,128)(2,1)} %get-tuple-element.101), channel_id=1, source_target_pairs={{0,64},{32,96},{64,0},{96,32},{1,65},{33,97},{65,1},{97,33},{2,66}... | collective-permute-start | bytes 884744 | tf_op jit(solution)/shard_map/exchange/y2/ppermute | solution.py:24
  17.6 14.0 %collective-permute-start.1 = (bf16[72,2048]{1,0:T(8,128)(2,1)S(1)}, bf16[72,2048]{1,0:T(8,128)(2,1)S(1)}, u32[]{:S(2)}, u32[]{:S(2)}) collective-permute-start(bf16[72,2048]{1,0:T(8,128)(2,1)S(1)} %get-tuple-element.100), channel_id=1, source_target_pairs={{0,32},{32,64},{64,96},{96,0},{1,33},{33,65},{65,97},{97,1},{2,34}... | collective-permute-start | bytes 884744 | tf_op jit(solution)/shard_map/exchange/y1/ppermute | solution.py:24
  20.0 148.3 %all-gather.5.cloned.1.call-start = ((), (), s32[]{:S(2)}) async-start(), calls=%async_computation.2 | async-start | bytes 10485760 | tf_op jit(solution)/shard_map/all_gather | solution.py:270
  23.4 8.8 %collective-permute-start.2 = (bf16[72,2048]{1,0:T(8,128)(2,1)S(1)}, bf16[72,2048]{1,0:T(8,128)(2,1)S(1)}, u32[]{:S(2)}, u32[]{:S(2)}) collective-permute-start(bf16[72,2048]{1,0:T(8,128)(2,1)S(1)} %get-tuple-element.99), channel_id=1, source_target_pairs={{0,96},{32,0},{64,32},{96,64},{1,97},{33,1},{65,33},{97,65},{2,98}... | collective-permute-start | bytes 884744 | tf_op jit(solution)/shard_map/exchange/y3/ppermute | solution.py:24
  34.2 21.4 %collective-permute-start.11 = (bf16[216,2048]{1,0:T(8,128)(2,1)S(1)}, bf16[216,2048]{1,0:T(8,128)(2,1)S(1)}, u32[]{:S(2)}, u32[]{:S(2)}) collective-permute-start(bf16[216,2048]{1,0:T(8,128)(2,1)S(1)} %pad_maximum_fusion.3.refs_0_), channel_id=1, source_target_pairs={{0,2},{2,4},{4,6},{6,0},{1,3},{3,5},{5,7},{7,1},{8,10},{10,12},{12... | collective-permute-start | bytes 2654216 | tf_op jit(solution)/shard_map/rest/x1/ppermute | solution.py:24
  34.3 21.5 %collective-permute-start.13 = (bf16[216,2048]{1,0:T(8,128)(2,1)S(1)}, bf16[216,2048]{1,0:T(8,128)(2,1)S(1)}, u32[]{:S(2)}, u32[]{:S(2)}) collective-permute-start(bf16[216,2048]{1,0:T(8,128)(2,1)S(1)} %pad_maximum_fusion.3.refs_0_), channel_id=1, source_target_pairs={{0,6},{2,0},{4,2},{6,4},{1,7},{3,1},{5,3},{7,5},{8,14},{10,8},{12,... | collective-permute-start | bytes 2654216 | tf_op jit(solution)/shard_map/rest/x3/ppermute | solution.py:24
  37.0 21.6 %collective-permute-start.10 = (bf16[1024,256]{1,0:T(8,128)(2,1)S(1)}, bf16[1024,256]{1,0:T(8,128)(2,1)S(1)}, u32[]{:S(2)}, u32[]{:S(2)}) collective-permute-start(bf16[1024,256]{1,0:T(8,128)(2,1)S(1)} %pad_maximum_fusion.11), channel_id=1, source_target_pairs={{0,96},{32,0},{64,32},{96,64},{1,97},{33,1},{65,33},{97,65},{2,98}... | collective-permute-start | bytes 1572872 | tf_op jit(solution)/shard_map/w_out/y3/ppermute | solution.py:24
  38.5 20.1 %collective-permute-start.8 = (bf16[1024,256]{1,0:T(8,128)(2,1)S(1)}, bf16[1024,256]{1,0:T(8,128)(2,1)S(1)}, u32[]{:S(2)}, u32[]{:S(2)}) collective-permute-start(bf16[1024,256]{1,0:T(8,128)(2,1)S(1)} %pad_maximum_fusion.11), channel_id=1, source_target_pairs={{0,32},{32,64},{64,96},{96,0},{1,33},{33,65},{65,97},{97,1},{2,34}... | collective-permute-start | bytes 1572872 | tf_op jit(solution)/shard_map/w_out/y1/ppermute | solution.py:24
  38.5 23.1 %collective-permute-start.9 = (bf16[1024,256]{1,0:T(8,128)(2,1)S(1)}, bf16[1024,256]{1,0:T(8,128)(2,1)S(1)}, u32[]{:S(2)}, u32[]{:S(2)}) collective-permute-start(bf16[1024,256]{1,0:T(8,128)(2,1)S(1)} %pad_maximum_fusion.11), channel_id=1, source_target_pairs={{0,64},{32,96},{64,0},{96,32},{1,65},{33,97},{65,1},{97,33},{2,66}... | collective-permute-start | bytes 1572872 | tf_op jit(solution)/shard_map/w_out/y2/ppermute | solution.py:24
  55.7 11.0 %collective-permute-start.12 = (bf16[216,1024]{1,0:T(8,128)(2,1)S(1)}, bf16[216,1024]{1,0:T(8,128)(2,1)S(1)}, u32[]{:S(2)}, u32[]{:S(2)}) collective-permute-start(bf16[216,1024]{1,0:T(8,128)(2,1)S(1)} %slice.250), channel_id=1, source_target_pairs={{0,2},{2,4},{4,6},{6,0},{1,3},{3,5},{5,7},{7,1},{8,10},{10,12},{12... | collective-permute-start | bytes 1327112 | tf_op jit(solution)/shard_map/rest/x1/ppermute | solution.py:24
  55.8 10.9 %collective-permute-start.14 = (bf16[216,1024]{1,0:T(8,128)(2,1)S(1)}, bf16[216,1024]{1,0:T(8,128)(2,1)}, u32[]{:S(2)}, u32[]{:S(2)}) collective-permute-start(bf16[216,1024]{1,0:T(8,128)(2,1)S(1)} %slice.251), channel_id=1, source_target_pairs={{0,6},{2,0},{4,2},{6,4},{1,7},{3,1},{5,3},{7,5},{8,14},{10,8},{12,... | collective-permute-start | bytes 1327112 | tf_op jit(solution)/shard_map/rest/x3/ppermute | solution.py:24
  68.4 13.1 %collective-permute-start.15 = (bf16[216,2048]{1,0:T(8,128)(2,1)S(1)}, bf16[216,2048]{1,0:T(8,128)(2,1)}, u32[]{:S(2)}, u32[]{:S(2)}) collective-permute-start(bf16[216,2048]{1,0:T(8,128)(2,1)S(1)} %pad_maximum_fusion.3.refs_0_), channel_id=1, source_target_pairs={{0,1},{1,0},{2,3},{3,2},{4,5},{5,4},{6,7},{7,6},{8,9},{9,8},{10,11... | collective-permute-start | bytes 2654216 | tf_op jit(solution)/shard_map/core/ppermute | solution.py:29
  71.3 10.2 %collective-permute-start.16 = (bf16[216,2048]{1,0:T(8,128)(2,1)S(1)}, bf16[216,2048]{1,0:T(8,128)(2,1)}, u32[]{:S(2)}, u32[]{:S(2)}) collective-permute-start(bf16[216,2048]{1,0:T(8,128)(2,1)S(1)} %collective-permute-done.11.refs_1_), channel_id=1, source_target_pairs={{0,1},{1,0},{2,3},{3,2},{4,5},{5,4},{6,7},{7,6},{8,9},{9,8},{10,11... | collective-permute-start | bytes 2654216 | tf_op jit(solution)/shard_map/rest/core/ppermute | solution.py:29
  71.4 10.1 %collective-permute-start.17 = (bf16[216,2048]{1,0:T(8,128)(2,1)S(1)}, bf16[216,2048]{1,0:T(8,128)(2,1)}, u32[]{:S(2)}, u32[]{:S(2)}) collective-permute-start(bf16[216,2048]{1,0:T(8,128)(2,1)S(1)} %collective-permute-done.13.refs_2_), channel_id=1, source_target_pairs={{0,1},{1,0},{2,3},{3,2},{4,5},{5,4},{6,7},{7,6},{8,9},{9,8},{10,11... | collective-permute-start | bytes 2654216 | tf_op jit(solution)/shard_map/rest/core/ppermute | solution.py:29
  86.7 19.9 %collective-permute-start.18 = (bf16[288,2048]{1,0:T(8,128)(2,1)S(1)}, bf16[288,2048]{1,0:T(8,128)(2,1)S(1)}, u32[]{:S(2)}, u32[]{:S(2)}) collective-permute-start(bf16[288,2048]{1,0:T(8,128)(2,1)S(1)} %pad_maximum_fusion.2), channel_id=1, source_target_pairs={{0,1},{1,0},{2,3},{3,2},{4,5},{5,4},{6,7},{7,6},{8,9},{9,8},{10,11... | collective-permute-start | bytes 3538952 | tf_op jit(solution)/shard_map/own/core/ppermute | solution.py:29
  90.3 11.5 %collective-permute-start.23 = (bf16[576,384]{1,0:T(8,128)(2,1)S(1)}, bf16[576,384]{1,0:T(8,128)(2,1)S(1)}, u32[]{:S(2)}, u32[]{:S(2)}) collective-permute-start(bf16[576,384]{1,0:T(8,128)(2,1)S(1)} %get-tuple-element.102), channel_id=1, source_target_pairs={{0,96},{32,0},{64,32},{96,64},{1,97},{33,1},{65,33},{97,65},{2,98}... | collective-permute-start | bytes 1327112 | tf_op jit(solution)/shard_map/y3/ppermute | solution.py:24
  92.2 12.9 %collective-permute-start.21 = (bf16[576,384]{1,0:T(8,128)(2,1)S(1)}, bf16[576,384]{1,0:T(8,128)(2,1)S(1)}, u32[]{:S(2)}, u32[]{:S(2)}) collective-permute-start(bf16[576,384]{1,0:T(8,128)(2,1)S(1)} %get-tuple-element.103), channel_id=1, source_target_pairs={{0,32},{32,64},{64,96},{96,0},{1,33},{33,65},{65,97},{97,1},{2,34}... | collective-permute-start | bytes 1327112 | tf_op jit(solution)/shard_map/y1/ppermute | solution.py:24
  101.9 20.9 %collective-permute-start.24 = (bf16[576,768]{1,0:T(8,128)(2,1)S(1)}, bf16[576,768]{1,0:T(8,128)(2,1)S(1)}, u32[]{:S(2)}, u32[]{:S(2)}) collective-permute-start(bf16[576,768]{1,0:T(8,128)(2,1)S(1)} %pad_maximum_fusion.5), channel_id=1, source_target_pairs={{0,96},{32,0},{64,32},{96,64},{1,97},{33,1},{65,33},{97,65},{2,98}... | collective-permute-start | bytes 2654216 | tf_op jit(solution)/shard_map/y3/ppermute | solution.py:24
  105.2 21.3 %collective-permute-start.22 = (bf16[576,768]{1,0:T(8,128)(2,1)S(1)}, bf16[576,768]{1,0:T(8,128)(2,1)S(1)}, u32[]{:S(2)}, u32[]{:S(2)}) collective-permute-start(bf16[576,768]{1,0:T(8,128)(2,1)S(1)} %pad_maximum_fusion.4), channel_id=1, source_target_pairs={{0,32},{32,64},{64,96},{96,0},{1,33},{33,65},{65,97},{97,1},{2,34}... | collective-permute-start | bytes 2654216 | tf_op jit(solution)/shard_map/y1/ppermute | solution.py:24
  133.9 21.3 %all-to-all-start = ((bf16[16,72,512]{2,1,0:T(8,128)(2,1)}), bf16[16,72,512]{2,1,0:T(8,128)(2,1)S(1)}, u32[]{:S(2)}, u32[]{:S(2)}) async-start(bf16[16,72,512]{2,1,0:T(8,128)(2,1)} %bitcast.12), calls=%async_computation | async-start | bytes 2359296 | tf_op jit(solution)/shard_map/all_to_all | solution.py:330
  173.4 10.6 %collective-permute-start.31 = (bf16[144,1024]{1,0:T(8,128)(2,1)S(1)}, bf16[144,1024]{1,0:T(8,128)(2,1)S(1)}, u32[]{:S(2)}, u32[]{:S(2)}) collective-permute-start(bf16[144,1024]{1,0:T(8,128)(2,1)S(1)} %get-tuple-element.88), channel_id=1, source_target_pairs={{0,2},{2,4},{4,6},{6,0},{1,3},{3,5},{5,7},{7,1},{8,10},{10,12},{12... | collective-permute-start | bytes 884744 | tf_op jit(solution)/shard_map/x1/ppermute | solution.py:24
  174.7 9.3 %collective-permute-start.33 = (bf16[144,1024]{1,0:T(8,128)(2,1)S(1)}, bf16[144,1024]{1,0:T(8,128)(2,1)S(1)}, u32[]{:S(2)}, u32[]{:S(2)}) collective-permute-start(bf16[144,1024]{1,0:T(8,128)(2,1)S(1)} %get-tuple-element.89), channel_id=1, source_target_pairs={{0,6},{2,0},{4,2},{6,4},{1,7},{3,1},{5,3},{7,5},{8,14},{10,8},{12,... | collective-permute-start | bytes 884744 | tf_op jit(solution)/shard_map/x3/ppermute | solution.py:24
  181.2 8.5 %collective-permute-start.26 = (bf16[144,1024]{1,0:T(8,128)(2,1)S(1)}, bf16[144,1024]{1,0:T(8,128)(2,1)S(1)}, u32[]{:S(2)}, u32[]{:S(2)}) collective-permute-start(bf16[144,1024]{1,0:T(8,128)(2,1)S(1)} %get-tuple-element.94), channel_id=1, source_target_pairs={{0,2},{2,4},{4,6},{6,0},{1,3},{3,5},{5,7},{7,1},{8,10},{10,12},{12... | collective-permute-start | bytes 884744 | tf_op jit(solution)/shard_map/x1/ppermute | solution.py:24
  181.3 8.4 %collective-permute-start.28 = (bf16[144,1024]{1,0:T(8,128)(2,1)S(1)}, bf16[144,1024]{1,0:T(8,128)(2,1)S(1)}, u32[]{:S(2)}, u32[]{:S(2)}) collective-permute-start(bf16[144,1024]{1,0:T(8,128)(2,1)S(1)} %get-tuple-element.95), channel_id=1, source_target_pairs={{0,6},{2,0},{4,2},{6,4},{1,7},{3,1},{5,3},{7,5},{8,14},{10,8},{12,... | collective-permute-start | bytes 884744 | tf_op jit(solution)/shard_map/x3/ppermute | solution.py:24
  184.3 18.1 %collective-permute-start.32 = (bf16[144,2048]{1,0:T(8,128)(2,1)S(1)}, bf16[144,2048]{1,0:T(8,128)(2,1)S(1)}, u32[]{:S(2)}, u32[]{:S(2)}) collective-permute-start(bf16[144,2048]{1,0:T(8,128)(2,1)S(1)} %pad_maximum_fusion.9), channel_id=1, source_target_pairs={{0,2},{2,4},{4,6},{6,0},{1,3},{3,5},{5,7},{7,1},{8,10},{10,12},{12... | collective-permute-start | bytes 1769480 | tf_op jit(solution)/shard_map/x1/ppermute | solution.py:24
  184.4 18.0 %collective-permute-start.34 = (bf16[144,2048]{1,0:T(8,128)(2,1)S(1)}, bf16[144,2048]{1,0:T(8,128)(2,1)S(1)}, u32[]{:S(2)}, u32[]{:S(2)}) collective-permute-start(bf16[144,2048]{1,0:T(8,128)(2,1)S(1)} %pad_maximum_fusion.10), channel_id=1, source_target_pairs={{0,6},{2,0},{4,2},{6,4},{1,7},{3,1},{5,3},{7,5},{8,14},{10,8},{12,... | collective-permute-start | bytes 1769480 | tf_op jit(solution)/shard_map/x3/ppermute | solution.py:24
  190.0 25.0 %collective-permute-start.27 = (bf16[144,2048]{1,0:T(8,128)(2,1)S(1)}, bf16[144,2048]{1,0:T(8,128)(2,1)S(1)}, u32[]{:S(2)}, u32[]{:S(2)}) collective-permute-start(bf16[144,2048]{1,0:T(8,128)(2,1)S(1)} %pad_maximum_fusion.7), channel_id=1, source_target_pairs={{0,2},{2,4},{4,6},{6,0},{1,3},{3,5},{5,7},{7,1},{8,10},{10,12},{12... | collective-permute-start | bytes 1769480 | tf_op jit(solution)/shard_map/x1/ppermute | solution.py:24
  190.2 24.9 %collective-permute-start.29 = (bf16[144,2048]{1,0:T(8,128)(2,1)S(1)}, bf16[144,2048]{1,0:T(8,128)(2,1)S(1)}, u32[]{:S(2)}, u32[]{:S(2)}) collective-permute-start(bf16[144,2048]{1,0:T(8,128)(2,1)S(1)} %pad_maximum_fusion.8), channel_id=1, source_target_pairs={{0,6},{2,0},{4,2},{6,4},{1,7},{3,1},{5,3},{7,5},{8,14},{10,8},{12,... | collective-permute-start | bytes 1769480 | tf_op jit(solution)/shard_map/x3/ppermute | solution.py:24
  203.4 15.4 %collective-permute-start.35 = (bf16[72,2048]{1,0:T(8,128)(2,1)S(1)}, bf16[72,2048]{1,0:T(8,128)(2,1)S(1)}, u32[]{:S(2)}, u32[]{:S(2)}) collective-permute-start(bf16[72,2048]{1,0:T(8,128)(2,1)S(1)} %get-tuple-element.120), channel_id=1, source_target_pairs={{0,1},{1,0},{2,3},{3,2},{4,5},{5,4},{6,7},{7,6},{8,9},{9,8},{10,11... | collective-permute-start | bytes 884744 | tf_op jit(solution)/shard_map/core/ppermute | solution.py:29
  (39 other events, 296.3 us)
Sparse Core Ops, SparseCore 0:
  20.1 39.8 all-gather.2
  68.5 99.7 all-gather.4

commit v3 on v1

--- a/solution.py
+++ b/solution.py
@@ -154,10 +154,12 @@
 def interleave_kernel(side, width, at_ref, *refs):
     *parts, out_ref = refs
     core, y = at_ref[0], at_ref[1]
-    blocks = parts[0].shape[1] // width
+    first = 0
     for j in range(len(parts) // 2):
+        blocks = parts[2 * j].shape[1] // width
+        first += parts[2 * j - 2].shape[1] // width if j else 0
         for i in range(blocks):
-            z, back = divmod(j * blocks + i, side)
+            z, back = divmod(first + i, side)
             at = lax.rem(y + side - back, side) * side + z
             for part, c in ((parts[2 * j], core), (parts[2 * j + 1], 1 - core)):
                 to = pl.multiple_of((at * 2 + c) * width, width)
@@ -165,11 +167,11 @@
 
 
 def interleave(side, width, at, parts):
-    rows, cols = parts[0].shape
+    rows, cols = parts[0].shape[0], sum(p.shape[1] for p in parts)
     vmem = pl.BlockSpec(memory_space=pltpu.VMEM)
     return pl.pallas_call(
         functools.partial(interleave_kernel, side, width),
-        out_shape=jax.ShapeDtypeStruct((rows, cols * len(parts)), BF),
+        out_shape=jax.ShapeDtypeStruct((rows, cols), BF),
         in_specs=[pl.BlockSpec(memory_space=pltpu.SMEM)] + [vmem] * len(parts),
         out_specs=vmem,
     )(at, *parts)
@@ -339,10 +341,9 @@
 
     parts = []
     pair = 2 * here
-    chunks = 2
-    count = packs // chunks
-    for j in range(chunks):
-        partial = project_out(j * count, count, moved, theirs, w_out)
+    short = packs // 4
+    for first, count in ((0, short), (short, packs - short)):
+        partial = project_out(first, count, moved, theirs, w_out)
         part = [partial[s * pair : (s + 1) * pair] for s in range(4)]
         mid = part[0].shape[1] // 2
         a = hop(part[2][:, :mid], "x", 1)

time: 225 us -> 231 us (1.027)
  waiting for transfers between devices: 93.6 us -> 98.6 us
    ppermute x26, waiting for transfers between devices: 75.1 us -> 80.4 us  [hop(): return lax.ppermute(v, axis, ring(lax.axis_size(axis), step))]
  transfers between devices with their start and end apart: 39 -> 39, of which waited for: 16 -> 16; matrix products, arithmetic and copies ran while one was open for 10% -> 10% of each run, Pallas kernels for 10% -> 9%
where the time goes in v3:
time: 231 us; the launch traced here: 230 us
  waiting for transfers between devices  98.6 us (43%)
  starting transfers between devices  57.5 us (25%)
  Pallas kernels  29.3 us (13%)
  other arithmetic  16.5 us (7%)
  between operations  14.4 us (6%)
  local copies, waits for them, and re-layouts  10.5 us (5%)
  matrix products  3.13 us (1%)
    ppermute x26, waiting for transfers between devices, hop(): return lax.ppermute(v, axis, ring(lax.axis_size(axis), step))  80.4 us
    ppermute x26, starting transfers between devices, hop(): return lax.ppermute(v, axis, ring(lax.axis_size(axis), step))  36.2 us
    all_to_all x1, waiting for transfers between devices, shards(): got = lax.all_to_all(sent, DP, split_axis=0, concat_axis=0, tiled=True)  16.1 us
    ppermute x10, starting transfers between devices, swap(): return lax.ppermute(v, 'c', [(0, 1), (1, 0)])  16.1 us
    pallas_call x2, Pallas kernels, project_out(): pl.pallas_call(project_out_kernel, out_shape=jax.ShapeDtypeStruct((rows,...  9.96 us
    pallas_call x4, Pallas kernels, multiply(): pl.pallas_call(functools.partial(multiply_kernel, [len(pieces) for pieces...  9.51 us
    pallas_call x1, Pallas kernels, attend(): pl.pallas_call(functools.partial(attend_kernel, here, heads), out_shape=j...  7.38 us
    unnamed x77, local copies, waits for them, and re-layouts  5.32 us
  transfers between devices with their start and end apart: 39, of which 16 were waited for; matrix products, arithmetic and copies ran while one was open for 10% of the time, Pallas kernels for 9%

profile of v3, /device:TPU:1, one launch (start us, length us, event | category | flops | bytes accessed | tf_op | source)
XLA Modules:
  0.0 230.0 jit_solution(18241623939988998490)
XLA Ops:
  7.6 2.0 pad_maximum_fusion.8
  11.5 2.0 collective-permute-start.3
  14.8 3.1 %collective-permute-start = (bf16[72,2048]{1,0:T(8,128)(2,1)}, bf16[72,2048]{1,0:T(8,128)(2,1)S(1)}, u32[]{:S(2)}, u32[]{:S(2)}) collective-permute-start(bf16[72,2048]{1,0:T(8,128)(2,1)} %get-tuple-element.91), channel_id=1, source_target_pairs={{0,64},{32,96},{64,0},{96,32},{1,65},{33,97},{65,1},{97,33},{2,66}... | collective-permute-start | bytes 884744 | tf_op jit(solution)/shard_map/exchange/y2/ppermute | solution.py:24
  23.5 2.4 %collective-permute-start.2 = (bf16[72,2048]{1,0:T(8,128)(2,1)}, bf16[72,2048]{1,0:T(8,128)(2,1)S(1)}, u32[]{:S(2)}, u32[]{:S(2)}) collective-permute-start(bf16[72,2048]{1,0:T(8,128)(2,1)} %get-tuple-element.89), channel_id=1, source_target_pairs={{0,96},{32,0},{64,32},{96,64},{1,97},{33,1},{65,33},{97,65},{2,98}... | collective-permute-start | bytes 884744 | tf_op jit(solution)/shard_map/exchange/y3/ppermute | solution.py:24
  28.0 2.7 %collective-permute-start.6 = (bf16[72,1024]{1,0:T(8,128)(2,1)S(1)}, bf16[72,1024]{1,0:T(8,128)(2,1)S(1)}, u32[]{:S(2)}, u32[]{:S(2)}) collective-permute-start(bf16[72,1024]{1,0:T(8,128)(2,1)S(1)} %slice.249), channel_id=1, source_target_pairs={{0,6},{2,0},{4,2},{6,4},{1,7},{3,1},{5,3},{7,5},{8,14},{10,8},{12,... | collective-permute-start | bytes 442376 | tf_op jit(solution)/shard_map/own/x3/ppermute | solution.py:24
  36.8 2.5 %collective-permute-start.13 = (bf16[1024,256]{1,0:T(8,128)(2,1)S(1)}, bf16[1024,256]{1,0:T(8,128)(2,1)S(1)}, u32[]{:S(2)}, u32[]{:S(2)}) collective-permute-start(bf16[1024,256]{1,0:T(8,128)(2,1)S(1)} %pad_maximum_fusion.9), channel_id=1, source_target_pairs={{0,64},{32,96},{64,0},{96,32},{1,65},{33,97},{65,1},{97,33},{2,66}... | collective-permute-start | bytes 1572872 | tf_op jit(solution)/shard_map/w_out/y2/ppermute | solution.py:24
  39.5 10.4 %collective-permute-done.12 = bf16[1024,256]{1,0:T(8,128)(2,1)S(1)} collective-permute-done((bf16[1024,256]{1,0:T(8,128)(2,1)S(1)}, bf16[1024,256]{1,0:T(8,128)(2,1)S(1)}, u32[]{:S(2)}, u32[]{:S(2)}) %collective-permute-start.12) | collective-permute-done | bytes 524320 | tf_op jit(solution)/shard_map/w_out/y1/ppermute | solution.py:24
  49.9 11.4 %collective-permute-done.13 = bf16[1024,256]{1,0:T(8,128)(2,1)S(1)} collective-permute-done((bf16[1024,256]{1,0:T(8,128)(2,1)S(1)}, bf16[1024,256]{1,0:T(8,128)(2,1)S(1)}, u32[]{:S(2)}, u32[]{:S(2)}) %collective-permute-start.13) | collective-permute-done | bytes 524320 | tf_op jit(solution)/shard_map/w_out/y2/ppermute | solution.py:24
  63.7 2.3 collective-permute-start.15
  68.2 2.7 %collective-permute-start.11 = (bf16[216,1024]{1,0:T(8,128)(2,1)}, bf16[216,1024]{1,0:T(8,128)(2,1)}, u32[]{:S(2)}, u32[]{:S(2)}) collective-permute-start(bf16[216,1024]{1,0:T(8,128)(2,1)} %slice.251), channel_id=1, source_target_pairs={{0,6},{2,0},{4,2},{6,4},{1,7},{3,1},{5,3},{7,5},{8,14},{10,8},{12,... | collective-permute-start | bytes 1327112 | tf_op jit(solution)/shard_map/rest/x3/ppermute | solution.py:24
  76.2 2.3 %copy-done = bf16[2048,768]{1,0:T(8,128)(2,1)S(1)} copy-done((bf16[2048,768]{1,0:T(8,128)(2,1)S(1)}, bf16[2048,768]{1,0:T(8,128)(2,1)}, u32[]{:S(2)}) %copy-start) | copy-done | bytes 3145752
  78.5 2.3 rest.4
  80.9 4.3 %rest.5 = (f32[216,768]{1,0:T(8,128)S(1)}, f32[216,768]{1,0:T(8,128)S(1)}, f32[216,768]{1,0:T(8,128)S(1)}) custom-call(bf16[2048,768]{1,0:T(8,128)(2,1)S(1)} %copy-done, bf16[216,2048]{1,0:T(8,128)(2,1)} %collective-permute-done.15.refs_0_, bf16[216,2048]{1,0:T(8,128)(2,1)} %collective-permute-done.16.refs_1_, bf16[216,2048]{1,0:T(8,128)(2,1)} %collective-permute-done.17.refs_2_), custom_call_target="tpu_custom_call" | custom-call | flops 1048576 | bytes 4096 | tf_op jit(solution)/shard_map/rest/pallas_call | solution.py:120
  86.6 2.0 rest.6
  90.0 2.1 collective-permute-start.23
  92.3 9.6 %collective-permute-done.23 = bf16[576,384]{1,0:T(8,128)(2,1)S(1)} collective-permute-done((bf16[576,384]{1,0:T(8,128)(2,1)S(1)}, bf16[576,384]{1,0:T(8,128)(2,1)S(1)}, u32[]{:S(2)}, u32[]{:S(2)}) %collective-permute-start.23) | collective-permute-done | bytes 442400 | tf_op jit(solution)/shard_map/y3/ppermute | solution.py:24
  102.1 3.3 %collective-permute-start.24 = (bf16[576,768]{1,0:T(8,128)(2,1)S(1)}, bf16[576,768]{1,0:T(8,128)(2,1)S(1)}, u32[]{:S(2)}, u32[]{:S(2)}) collective-permute-start(bf16[576,768]{1,0:T(8,128)(2,1)S(1)} %pad_maximum_fusion.5), channel_id=1, source_target_pairs={{0,96},{32,0},{64,32},{96,64},{1,97},{33,1},{65,33},{97,65},{2,98}... | collective-permute-start | bytes 2654216 | tf_op jit(solution)/shard_map/y3/ppermute | solution.py:24
  108.3 15.4 %collective-permute-done.24.p_ref = bf16[576,768]{1,0:T(8,128)(2,1)S(1)} collective-permute-done((bf16[576,768]{1,0:T(8,128)(2,1)S(1)}, bf16[576,768]{1,0:T(8,128)(2,1)S(1)}, u32[]{:S(2)}, u32[]{:S(2)}) %collective-permute-start.24) | collective-permute-done | bytes 884768 | tf_op jit(solution)/shard_map/y3/ppermute | solution.py:24
  123.7 3.7 %collective-permute-done.22.m_ref = bf16[576,768]{1,0:T(8,128)(2,1)S(1)} collective-permute-done((bf16[576,768]{1,0:T(8,128)(2,1)S(1)}, bf16[576,768]{1,0:T(8,128)(2,1)S(1)}, u32[]{:S(2)}, u32[]{:S(2)}) %collective-permute-start.22) | collective-permute-done | bytes 884768 | tf_op jit(solution)/shard_map/y1/ppermute | solution.py:24
  127.4 7.4 %shard_map.100 = bf16[1152,512]{1,0:T(8,128)(2,1)} custom-call(s32[1]{0:T(128)} %bitcast.core_ref, f32[576,768]{1,0:T(8,128)S(1)} %pad_maximum_fusion.1.sum_ref, bf16[576,768]{1,0:T(8,128)(2,1)S(1)} %collective-permute-done.22.m_ref, bf16[576,768]{1,0:T(8,128)(2,1)S(1)} %collective-permute-done.24.p_ref, f32[1,768]{1,0:T(1,128)S(1)} %broadcast_in_dim.14.bias_ref, ...), custom_call_target="tpu_custom_call" | custom-call | flops 1073741824 | bytes 8388608 | tf_op jit(solution)/shard_map/pallas_call | solution.py:87
  134.7 5.1 %all-to-all-start = ((bf16[16,72,512]{2,1,0:T(8,128)(2,1)}), bf16[16,72,512]{2,1,0:T(8,128)(2,1)S(1)}, u32[]{:S(2)}, u32[]{:S(2)}) async-start(bf16[16,72,512]{2,1,0:T(8,128)(2,1)} %bitcast.16), calls=%async_computation | async-start | bytes 2359296 | tf_op jit(solution)/shard_map/all_to_all | solution.py:332
  139.9 16.1 %all-to-all-done = bf16[16,72,512]{2,1,0:T(8,128)(2,1)S(1)} async-done(((bf16[16,72,512]{2,1,0:T(8,128)(2,1)}), bf16[16,72,512]{2,1,0:T(8,128)(2,1)S(1)}, u32[]{:S(2)}, u32[]{:S(2)}) %all-to-all-start) | async-done | bytes 1179680 | tf_op jit(solution)/shard_map/all_to_all | solution.py:332
  157.0 4.1 %collective-permute-start.25 = (bf16[576,512]{1,0:T(8,128)(2,1)S(1)}, bf16[576,512]{1,0:T(8,128)(2,1)S(1)}, u32[]{:S(2)}, u32[]{:S(2)}) collective-permute-start(bf16[576,512]{1,0:T(8,128)(2,1)S(1)} %fusion.5.mine_ref), channel_id=1, source_target_pairs={{0,1},{1,0},{2,3},{3,2},{4,5},{5,4},{6,7},{7,6},{8,9},{9,8},{10,11... | collective-permute-start | bytes 1769480 | tf_op jit(solution)/shard_map/core/ppermute | solution.py:29
  162.8 7.1 %shard_map.102 = bf16[576,3072]{1,0:T(8,128)(2,1)S(1)} custom-call(bf16[576,512]{1,0:T(8,128)(2,1)S(1)} %fusion.5.mine_ref, bf16[576,512]{1,0:T(8,128)(2,1)S(1)} %collective-permute-done.25.theirs_ref, bf16[16,1024,256]{2,1,0:T(8,128)(2,1)} %all-gather.5.cloned.1.call-done.w_ref), custom_call_target="tpu_custom_call" | custom-call | flops 3623878656 | bytes 8388608 | tf_op jit(solution)/shard_map/pallas_call | solution.py:141
  173.1 9.6 %collective-permute-done.31 = bf16[144,1536]{1,0:T(8,128)(2,1)S(1)} collective-permute-done((bf16[144,1536]{1,0:T(8,128)(2,1)S(1)}, bf16[144,1536]{1,0:T(8,128)(2,1)S(1)}, u32[]{:S(2)}, u32[]{:S(2)}) %collective-permute-start.31) | collective-permute-done | bytes 442400 | tf_op jit(solution)/shard_map/x1/ppermute | solution.py:24
  183.7 2.2 collective-permute-start.34
  185.9 2.9 %shard_map.101 = bf16[576,1024]{1,0:T(8,128)(2,1)S(1)} custom-call(bf16[576,512]{1,0:T(8,128)(2,1)S(1)} %fusion.5.mine_ref, bf16[576,512]{1,0:T(8,128)(2,1)S(1)} %collective-permute-done.25.theirs_ref, bf16[16,1024,256]{2,1,0:T(8,128)(2,1)} %all-gather.5.cloned.1.call-done.w_ref), custom_call_target="tpu_custom_call" | custom-call | flops 1207959552 | bytes 8388608 | tf_op jit(solution)/shard_map/pallas_call | solution.py:141
  188.9 2.7 %collective-permute-start.28 = (bf16[144,512]{1,0:T(8,128)(2,1)S(1)}, bf16[144,512]{1,0:T(8,128)(2,1)S(1)}, u32[]{:S(2)}, u32[]{:S(2)}) collective-permute-start(bf16[144,512]{1,0:T(8,128)(2,1)S(1)} %get-tuple-element.85), channel_id=1, source_target_pairs={{0,6},{2,0},{4,2},{6,4},{1,7},{3,1},{5,3},{7,5},{8,14},{10,8},{12,... | collective-permute-start | bytes 442376 | tf_op jit(solution)/shard_map/x3/ppermute | solution.py:24
  191.6 15.6 %collective-permute-done.26 = bf16[144,512]{1,0:T(8,128)(2,1)S(1)} collective-permute-done((bf16[144,512]{1,0:T(8,128)(2,1)S(1)}, bf16[144,512]{1,0:T(8,128)(2,1)S(1)}, u32[]{:S(2)}, u32[]{:S(2)}) %collective-permute-start.26) | collective-permute-done | bytes 147488 | tf_op jit(solution)/shard_map/x1/ppermute | solution.py:24
  211.4 2.9 %collective-permute-start.35 = (bf16[72,3072]{1,0:T(8,128)(2,1)S(1)}, bf16[72,3072]{1,0:T(8,128)(2,1)S(1)}, u32[]{:S(2)}, u32[]{:S(2)}) collective-permute-start(bf16[72,3072]{1,0:T(8,128)(2,1)S(1)} %get-tuple-element.92), channel_id=1, source_target_pairs={{0,1},{1,0},{2,3},{3,2},{4,5},{5,4},{6,7},{7,6},{8,9},{9,8},{10,11... | collective-permute-start | bytes 1327112 | tf_op jit(solution)/shard_map/core/ppermute | solution.py:29
  215.6 3.3 %collective-permute-start.30 = (bf16[72,1024]{1,0:T(8,128)(2,1)S(1)}, bf16[72,1024]{1,0:T(8,128)(2,1)S(1)}, u32[]{:S(2)}, u32[]{:S(2)}) collective-permute-start(bf16[72,1024]{1,0:T(8,128)(2,1)S(1)} %get-tuple-element.114), channel_id=1, source_target_pairs={{0,1},{1,0},{2,3},{3,2},{4,5},{5,4},{6,7},{7,6},{8,9},{9,8},{10,11... | collective-permute-start | bytes 442376 | tf_op jit(solution)/shard_map/core/ppermute | solution.py:29
  220.7 2.5 %shard_map.103 = bf16[72,8192]{1,0:T(8,128)(2,1)} custom-call(s32[2]{0:T(128)} %pad_add_fusion.at_ref, bf16[72,1024]{1,0:T(8,128)(2,1)} %get-tuple-element.115.refs_0_, bf16[72,1024]{1,0:T(8,128)(2,1)} %copy-done.17, bf16[72,3072]{1,0:T(8,128)(2,1)} %get-tuple-element.93.refs_2_, bf16[72,3072]{1,0:T(8,128)(2,1)} %copy-done.11), custom_call_target="tpu_custom_call" | custom-call | tf_op jit(solution)/shard_map/pallas_call | solution.py:172
  (214 shorter events, 47.6 us)
Async XLA Ops:
  6.5 69.7 %all-gather.3.cloned.1.call-start = ((), (), s32[]{:S(2)}) async-start(), calls=%async_computation.1 | async-start | bytes 3932160 | tf_op jit(solution)/shard_map/all_gather | solution.py:235
  9.6 153.2 %all-gather.5.cloned.1.call-start = ((), (), s32[]{:S(2)}) async-start(), calls=%async_computation.2 | async-start | bytes 10485760 | tf_op jit(solution)/shard_map/all_gather | solution.py:272
  11.5 16.4 %collective-permute-start.3 = (bf16[72,2048]{1,0:T(8,128)(2,1)S(1)}, bf16[72,2048]{1,0:T(8,128)(2,1)S(1)}, u32[]{:S(2)}, u32[]{:S(2)}) collective-permute-start(bf16[72,2048]{1,0:T(8,128)(2,1)S(1)} %get-tuple-element.53), channel_id=1, source_target_pairs={{0,2},{2,4},{4,6},{6,0},{1,3},{3,5},{5,7},{7,1},{8,10},{10,12},{12... | collective-permute-start | bytes 884744 | tf_op jit(solution)/shard_map/own/x1/ppermute | solution.py:24
  13.5 14.5 %collective-permute-start.4 = (bf16[72,2048]{1,0:T(8,128)(2,1)S(1)}, bf16[72,2048]{1,0:T(8,128)(2,1)S(1)}, u32[]{:S(2)}, u32[]{:S(2)}) collective-permute-start(bf16[72,2048]{1,0:T(8,128)(2,1)S(1)} %get-tuple-element.53), channel_id=1, source_target_pairs={{0,6},{2,0},{4,2},{6,4},{1,7},{3,1},{5,3},{7,5},{8,14},{10,8},{12,... | collective-permute-start | bytes 884744 | tf_op jit(solution)/shard_map/own/x3/ppermute | solution.py:24
  14.8 16.0 %collective-permute-start = (bf16[72,2048]{1,0:T(8,128)(2,1)}, bf16[72,2048]{1,0:T(8,128)(2,1)S(1)}, u32[]{:S(2)}, u32[]{:S(2)}) collective-permute-start(bf16[72,2048]{1,0:T(8,128)(2,1)} %get-tuple-element.91), channel_id=1, source_target_pairs={{0,64},{32,96},{64,0},{96,32},{1,65},{33,97},{65,1},{97,33},{2,66}... | collective-permute-start | bytes 884744 | tf_op jit(solution)/shard_map/exchange/y2/ppermute | solution.py:24
  17.9 14.1 %collective-permute-start.1 = (bf16[72,2048]{1,0:T(8,128)(2,1)}, bf16[72,2048]{1,0:T(8,128)(2,1)S(1)}, u32[]{:S(2)}, u32[]{:S(2)}) collective-permute-start(bf16[72,2048]{1,0:T(8,128)(2,1)} %get-tuple-element.90), channel_id=1, source_target_pairs={{0,32},{32,64},{64,96},{96,0},{1,33},{33,65},{65,97},{97,1},{2,34}... | collective-permute-start | bytes 884744 | tf_op jit(solution)/shard_map/exchange/y1/ppermute | solution.py:24
  23.5 9.0 %collective-permute-start.2 = (bf16[72,2048]{1,0:T(8,128)(2,1)}, bf16[72,2048]{1,0:T(8,128)(2,1)S(1)}, u32[]{:S(2)}, u32[]{:S(2)}) collective-permute-start(bf16[72,2048]{1,0:T(8,128)(2,1)} %get-tuple-element.89), channel_id=1, source_target_pairs={{0,96},{32,0},{64,32},{96,64},{1,97},{33,1},{65,33},{97,65},{2,98}... | collective-permute-start | bytes 884744 | tf_op jit(solution)/shard_map/exchange/y3/ppermute | solution.py:24
  28.0 7.0 %collective-permute-start.6 = (bf16[72,1024]{1,0:T(8,128)(2,1)S(1)}, bf16[72,1024]{1,0:T(8,128)(2,1)S(1)}, u32[]{:S(2)}, u32[]{:S(2)}) collective-permute-start(bf16[72,1024]{1,0:T(8,128)(2,1)S(1)} %slice.249), channel_id=1, source_target_pairs={{0,6},{2,0},{4,2},{6,4},{1,7},{3,1},{5,3},{7,5},{8,14},{10,8},{12,... | collective-permute-start | bytes 442376 | tf_op jit(solution)/shard_map/own/x3/ppermute | solution.py:24
  35.0 28.6 %collective-permute-start.10 = (bf16[216,2048]{1,0:T(8,128)(2,1)S(1)}, bf16[216,2048]{1,0:T(8,128)(2,1)S(1)}, u32[]{:S(2)}, u32[]{:S(2)}) collective-permute-start(bf16[216,2048]{1,0:T(8,128)(2,1)S(1)} %pad_maximum_fusion.3.refs_0_), channel_id=1, source_target_pairs={{0,6},{2,0},{4,2},{6,4},{1,7},{3,1},{5,3},{7,5},{8,14},{10,8},{12,... | collective-permute-start | bytes 2654216 | tf_op jit(solution)/shard_map/rest/x3/ppermute | solution.py:24
  36.8 26.8 %collective-permute-start.8 = (bf16[216,2048]{1,0:T(8,128)(2,1)S(1)}, bf16[216,2048]{1,0:T(8,128)(2,1)S(1)}, u32[]{:S(2)}, u32[]{:S(2)}) collective-permute-start(bf16[216,2048]{1,0:T(8,128)(2,1)S(1)} %pad_maximum_fusion.3.refs_0_), channel_id=1, source_target_pairs={{0,2},{2,4},{4,6},{6,0},{1,3},{3,5},{5,7},{7,1},{8,10},{10,12},{12... | collective-permute-start | bytes 2654216 | tf_op jit(solution)/shard_map/rest/x1/ppermute | solution.py:24
  36.8 13.0 %collective-permute-start.12 = (bf16[1024,256]{1,0:T(8,128)(2,1)S(1)}, bf16[1024,256]{1,0:T(8,128)(2,1)S(1)}, u32[]{:S(2)}, u32[]{:S(2)}) collective-permute-start(bf16[1024,256]{1,0:T(8,128)(2,1)S(1)} %pad_maximum_fusion.9), channel_id=1, source_target_pairs={{0,32},{32,64},{64,96},{96,0},{1,33},{33,65},{65,97},{97,1},{2,34}... | collective-permute-start | bytes 1572872 | tf_op jit(solution)/shard_map/w_out/y1/ppermute | solution.py:24
  36.8 24.4 %collective-permute-start.13 = (bf16[1024,256]{1,0:T(8,128)(2,1)S(1)}, bf16[1024,256]{1,0:T(8,128)(2,1)S(1)}, u32[]{:S(2)}, u32[]{:S(2)}) collective-permute-start(bf16[1024,256]{1,0:T(8,128)(2,1)S(1)} %pad_maximum_fusion.9), channel_id=1, source_target_pairs={{0,64},{32,96},{64,0},{96,32},{1,65},{33,97},{65,1},{97,33},{2,66}... | collective-permute-start | bytes 1572872 | tf_op jit(solution)/shard_map/w_out/y2/ppermute | solution.py:24
  39.4 22.7 %collective-permute-start.14 = (bf16[1024,256]{1,0:T(8,128)(2,1)S(1)}, bf16[1024,256]{1,0:T(8,128)(2,1)S(1)}, u32[]{:S(2)}, u32[]{:S(2)}) collective-permute-start(bf16[1024,256]{1,0:T(8,128)(2,1)S(1)} %pad_maximum_fusion.9), channel_id=1, source_target_pairs={{0,96},{32,0},{64,32},{96,64},{1,97},{33,1},{65,33},{97,65},{2,98}... | collective-permute-start | bytes 1572872 | tf_op jit(solution)/shard_map/w_out/y3/ppermute | solution.py:24
  63.7 17.2 %collective-permute-start.15 = (bf16[216,2048]{1,0:T(8,128)(2,1)S(1)}, bf16[216,2048]{1,0:T(8,128)(2,1)}, u32[]{:S(2)}, u32[]{:S(2)}) collective-permute-start(bf16[216,2048]{1,0:T(8,128)(2,1)S(1)} %pad_maximum_fusion.3.refs_0_), channel_id=1, source_target_pairs={{0,1},{1,0},{2,3},{3,2},{4,5},{5,4},{6,7},{7,6},{8,9},{9,8},{10,11... | collective-permute-start | bytes 2654216 | tf_op jit(solution)/shard_map/core/ppermute | solution.py:29
  66.0 14.9 %collective-permute-start.16 = (bf16[216,2048]{1,0:T(8,128)(2,1)S(1)}, bf16[216,2048]{1,0:T(8,128)(2,1)}, u32[]{:S(2)}, u32[]{:S(2)}) collective-permute-start(bf16[216,2048]{1,0:T(8,128)(2,1)S(1)} %collective-permute-done.8.refs_1_), channel_id=1, source_target_pairs={{0,1},{1,0},{2,3},{3,2},{4,5},{5,4},{6,7},{7,6},{8,9},{9,8},{10,11... | collective-permute-start | bytes 2654216 | tf_op jit(solution)/shard_map/rest/core/ppermute | solution.py:29
  66.1 14.8 %collective-permute-start.17 = (bf16[216,2048]{1,0:T(8,128)(2,1)S(1)}, bf16[216,2048]{1,0:T(8,128)(2,1)}, u32[]{:S(2)}, u32[]{:S(2)}) collective-permute-start(bf16[216,2048]{1,0:T(8,128)(2,1)S(1)} %collective-permute-done.10.refs_2_), channel_id=1, source_target_pairs={{0,1},{1,0},{2,3},{3,2},{4,5},{5,4},{6,7},{7,6},{8,9},{9,8},{10,11... | collective-permute-start | bytes 2654216 | tf_op jit(solution)/shard_map/rest/core/ppermute | solution.py:29
  68.2 17.0 %collective-permute-start.11 = (bf16[216,1024]{1,0:T(8,128)(2,1)}, bf16[216,1024]{1,0:T(8,128)(2,1)}, u32[]{:S(2)}, u32[]{:S(2)}) collective-permute-start(bf16[216,1024]{1,0:T(8,128)(2,1)} %slice.251), channel_id=1, source_target_pairs={{0,6},{2,0},{4,2},{6,4},{1,7},{3,1},{5,3},{7,5},{8,14},{10,8},{12,... | collective-permute-start | bytes 1327112 | tf_op jit(solution)/shard_map/rest/x3/ppermute | solution.py:24
  71.7 13.6 %collective-permute-start.9 = (bf16[216,1024]{1,0:T(8,128)(2,1)}, bf16[216,1024]{1,0:T(8,128)(2,1)}, u32[]{:S(2)}, u32[]{:S(2)}) collective-permute-start(bf16[216,1024]{1,0:T(8,128)(2,1)} %slice.250), channel_id=1, source_target_pairs={{0,2},{2,4},{4,6},{6,0},{1,3},{3,5},{5,7},{7,1},{8,10},{10,12},{12... | collective-permute-start | bytes 1327112 | tf_op jit(solution)/shard_map/rest/x1/ppermute | solution.py:24
  86.0 21.0 %collective-permute-start.18 = (bf16[288,2048]{1,0:T(8,128)(2,1)S(1)}, bf16[288,2048]{1,0:T(8,128)(2,1)S(1)}, u32[]{:S(2)}, u32[]{:S(2)}) collective-permute-start(bf16[288,2048]{1,0:T(8,128)(2,1)S(1)} %pad_maximum_fusion.2), channel_id=1, source_target_pairs={{0,1},{1,0},{2,3},{3,2},{4,5},{5,4},{6,7},{7,6},{8,9},{9,8},{10,11... | collective-permute-start | bytes 3538952 | tf_op jit(solution)/shard_map/own/core/ppermute | solution.py:29
  90.0 11.9 %collective-permute-start.23 = (bf16[576,384]{1,0:T(8,128)(2,1)S(1)}, bf16[576,384]{1,0:T(8,128)(2,1)S(1)}, u32[]{:S(2)}, u32[]{:S(2)}) collective-permute-start(bf16[576,384]{1,0:T(8,128)(2,1)S(1)} %get-tuple-element.94), channel_id=1, source_target_pairs={{0,96},{32,0},{64,32},{96,64},{1,97},{33,1},{65,33},{97,65},{2,98}... | collective-permute-start | bytes 1327112 | tf_op jit(solution)/shard_map/y3/ppermute | solution.py:24
  92.1 13.3 %collective-permute-start.21 = (bf16[576,384]{1,0:T(8,128)(2,1)S(1)}, bf16[576,384]{1,0:T(8,128)(2,1)S(1)}, u32[]{:S(2)}, u32[]{:S(2)}) collective-permute-start(bf16[576,384]{1,0:T(8,128)(2,1)S(1)} %get-tuple-element.95), channel_id=1, source_target_pairs={{0,32},{32,64},{64,96},{96,0},{1,33},{33,65},{65,97},{97,1},{2,34}... | collective-permute-start | bytes 1327112 | tf_op jit(solution)/shard_map/y1/ppermute | solution.py:24
  102.1 21.6 %collective-permute-start.24 = (bf16[576,768]{1,0:T(8,128)(2,1)S(1)}, bf16[576,768]{1,0:T(8,128)(2,1)S(1)}, u32[]{:S(2)}, u32[]{:S(2)}) collective-permute-start(bf16[576,768]{1,0:T(8,128)(2,1)S(1)} %pad_maximum_fusion.5), channel_id=1, source_target_pairs={{0,96},{32,0},{64,32},{96,64},{1,97},{33,1},{65,33},{97,65},{2,98}... | collective-permute-start | bytes 2654216 | tf_op jit(solution)/shard_map/y3/ppermute | solution.py:24
  105.6 21.7 %collective-permute-start.22 = (bf16[576,768]{1,0:T(8,128)(2,1)S(1)}, bf16[576,768]{1,0:T(8,128)(2,1)S(1)}, u32[]{:S(2)}, u32[]{:S(2)}) collective-permute-start(bf16[576,768]{1,0:T(8,128)(2,1)S(1)} %pad_maximum_fusion.4), channel_id=1, source_target_pairs={{0,32},{32,64},{64,96},{96,0},{1,33},{33,65},{65,97},{97,1},{2,34}... | collective-permute-start | bytes 2654216 | tf_op jit(solution)/shard_map/y1/ppermute | solution.py:24
  134.7 21.3 %all-to-all-start = ((bf16[16,72,512]{2,1,0:T(8,128)(2,1)}), bf16[16,72,512]{2,1,0:T(8,128)(2,1)S(1)}, u32[]{:S(2)}, u32[]{:S(2)}) async-start(bf16[16,72,512]{2,1,0:T(8,128)(2,1)} %bitcast.16), calls=%async_computation | async-start | bytes 2359296 | tf_op jit(solution)/shard_map/all_to_all | solution.py:332
  170.1 12.6 %collective-permute-start.31 = (bf16[144,1536]{1,0:T(8,128)(2,1)S(1)}, bf16[144,1536]{1,0:T(8,128)(2,1)S(1)}, u32[]{:S(2)}, u32[]{:S(2)}) collective-permute-start(bf16[144,1536]{1,0:T(8,128)(2,1)S(1)} %get-tuple-element.78), channel_id=1, source_target_pairs={{0,2},{2,4},{4,6},{6,0},{1,3},{3,5},{5,7},{7,1},{8,10},{10,12},{12... | collective-permute-start | bytes 1327112 | tf_op jit(solution)/shard_map/x1/ppermute | solution.py:24
  171.4 11.3 %collective-permute-start.33 = (bf16[144,1536]{1,0:T(8,128)(2,1)S(1)}, bf16[144,1536]{1,0:T(8,128)(2,1)S(1)}, u32[]{:S(2)}, u32[]{:S(2)}) collective-permute-start(bf16[144,1536]{1,0:T(8,128)(2,1)S(1)} %get-tuple-element.79), channel_id=1, source_target_pairs={{0,6},{2,0},{4,2},{6,4},{1,7},{3,1},{5,3},{7,5},{8,14},{10,8},{12,... | collective-permute-start | bytes 1327112 | tf_op jit(solution)/shard_map/x3/ppermute | solution.py:24
  183.0 27.1 %collective-permute-start.32 = (bf16[144,3072]{1,0:T(8,128)(2,1)S(1)}, bf16[144,3072]{1,0:T(8,128)(2,1)S(1)}, u32[]{:S(2)}, u32[]{:S(2)}) collective-permute-start(bf16[144,3072]{1,0:T(8,128)(2,1)S(1)} %pad_maximum_fusion.6), channel_id=1, source_target_pairs={{0,2},{2,4},{4,6},{6,0},{1,3},{3,5},{5,7},{7,1},{8,10},{10,12},{12... | collective-permute-start | bytes 2654216 | tf_op jit(solution)/shard_map/x1/ppermute | solution.py:24
  183.7 26.4 %collective-permute-start.34 = (bf16[144,3072]{1,0:T(8,128)(2,1)S(1)}, bf16[144,3072]{1,0:T(8,128)(2,1)S(1)}, u32[]{:S(2)}, u32[]{:S(2)}) collective-permute-start(bf16[144,3072]{1,0:T(8,128)(2,1)S(1)} %pad_maximum_fusion.7), channel_id=1, source_target_pairs={{0,6},{2,0},{4,2},{6,4},{1,7},{3,1},{5,3},{7,5},{8,14},{10,8},{12,... | collective-permute-start | bytes 2654216 | tf_op jit(solution)/shard_map/x3/ppermute | solution.py:24
  188.8 18.3 %collective-permute-start.26 = (bf16[144,512]{1,0:T(8,128)(2,1)S(1)}, bf16[144,512]{1,0:T(8,128)(2,1)S(1)}, u32[]{:S(2)}, u32[]{:S(2)}) collective-permute-start(bf16[144,512]{1,0:T(8,128)(2,1)S(1)} %get-tuple-element.84), channel_id=1, source_target_pairs={{0,2},{2,4},{4,6},{6,0},{1,3},{3,5},{5,7},{7,1},{8,10},{10,12},{12... | collective-permute-start | bytes 442376 | tf_op jit(solution)/shard_map/x1/ppermute | solution.py:24
  188.9 18.2 %collective-permute-start.28 = (bf16[144,512]{1,0:T(8,128)(2,1)S(1)}, bf16[144,512]{1,0:T(8,128)(2,1)S(1)}, u32[]{:S(2)}, u32[]{:S(2)}) collective-permute-start(bf16[144,512]{1,0:T(8,128)(2,1)S(1)} %get-tuple-element.85), channel_id=1, source_target_pairs={{0,6},{2,0},{4,2},{6,4},{1,7},{3,1},{5,3},{7,5},{8,14},{10,8},{12,... | collective-permute-start | bytes 442376 | tf_op jit(solution)/shard_map/x3/ppermute | solution.py:24
  207.3 7.4 %collective-permute-start.27 = (bf16[144,1024]{1,0:T(8,128)(2,1)S(1)}, bf16[144,1024]{1,0:T(8,128)(2,1)S(1)}, u32[]{:S(2)}, u32[]{:S(2)}) collective-permute-start(bf16[144,1024]{1,0:T(8,128)(2,1)S(1)} %pad_maximum_fusion.12), channel_id=1, source_target_pairs={{0,2},{2,4},{4,6},{6,0},{1,3},{3,5},{5,7},{7,1},{8,10},{10,12},{12... | collective-permute-start | bytes 884744 | tf_op jit(solution)/shard_map/x1/ppermute | solution.py:24
  211.4 8.5 %collective-permute-start.35 = (bf16[72,3072]{1,0:T(8,128)(2,1)S(1)}, bf16[72,3072]{1,0:T(8,128)(2,1)S(1)}, u32[]{:S(2)}, u32[]{:S(2)}) collective-permute-start(bf16[72,3072]{1,0:T(8,128)(2,1)S(1)} %get-tuple-element.92), channel_id=1, source_target_pairs={{0,1},{1,0},{2,3},{3,2},{4,5},{5,4},{6,7},{7,6},{8,9},{9,8},{10,11... | collective-permute-start | bytes 1327112 | tf_op jit(solution)/shard_map/core/ppermute | solution.py:29
  (38 other events, 236.0 us)
Sparse Core Ops, SparseCore 0:
  9.8 42.9 all-gather.2
  63.8 98.9 all-gather.4
